TPU v7x, 512 devices: a whole 4x8x8 slice. The times are simulated.
512 devices in a mesh: gz: 64 (over y_hi, x, z), af: 8 (over y_lo, core).
Axes of the slice: x: 4, y: 8 (y_hi: 2, y_lo: 4; y = y_hi * 4 + y_lo), z: 8, core: 2. Of those that a mesh axis runs over, the one named last changes fastest.
Arguments:
- inputs: bfloat16 [256, 64, 8, 128], P('af', 'gz'), may hold values from -6 to 6
- pre_acts: bfloat16 [256, 64, 8, 128], P('af', 'gz'), may hold values from -6 to 6
- out_grad: bfloat16 [256, 64, 8, 128], P('af', 'gz'), may hold values from -4 to 4
- weight_one: bfloat16 [256, 27, 256], P('af'), may hold values from -0.078125 to 0.078125
- weight_two: bfloat16 [256, 27, 256], P('af'), may hold values from -0.078125 to 0.078125
Outputs:
- input_grad: bfloat16 [256, 64, 8, 128], P('af', 'gz')
- filter_grad_one: float32 [27, 256, 256], P(None, 'gz', 'af')
- filter_grad_two: float32 [27, 256, 256], P(None, 'gz', 'af')
All inputs are finite; a program needn't handle non-finite values.
Results may differ from a plain program's by a relative error of at most 0.0049.
Values may be sent and summed in bfloat16 or wider, within the bound.
A program may use at most 128 MiB of HBM per device.

v0:
```python
import jax
import jax.numpy as jnp
from jax import lax
from jax.sharding import PartitionSpec as P

tap_offsets = [(a, b, c) for a in (-1, 0, 1) for b in (-1, 0, 1) for c in (-1, 0, 1)]
contract_last = (((1,), (1,)), ((), ()))


def with_halo(cells, sides, width):
    for axis, dim in sides:
        count = lax.axis_size(axis)
        ends = count - 1
        head = lax.slice_in_dim(cells, 0, width, axis=dim)
        tail = lax.slice_in_dim(cells, cells.shape[dim] - width, cells.shape[dim], axis=dim)
        cells = jnp.concatenate(
            [
                lax.ppermute(tail, axis, [(i, (i + 1) % count) for i in range(ends)]),
                cells,
                lax.ppermute(head, axis, [((i + 1) % count, i) for i in range(ends)]),
            ],
            axis=dim,
        )
    return cells


def tap_cells(padded, offset, planes, height, across):
    return padded[
        :,
        1 - offset[0] : 1 - offset[0] + planes,
        1 - offset[1] : 1 - offset[1] + height,
        1 - offset[2] : 1 - offset[2] + across,
    ]


def pad_plane(values):
    return jnp.pad(values, ((0, 0), (0, 0), (1, 1), (1, 1)))


def layer_back(activation, gradient, weight):
    own_channels, planes, height, across = gradient.shape
    channels = weight.shape[2]
    cell_count = planes * height * across
    grad_padded = pad_plane(with_halo(gradient, (("gz", 1),), 1))
    stacked = jnp.concatenate(
        [tap_cells(grad_padded, offset, planes, height, across) for offset in tap_offsets], axis=0
    )
    stacked = stacked.reshape(27 * own_channels, cell_count)
    act_padded = pad_plane(with_halo(activation, (("gz", 1),), 1))
    flat_grad = gradient.reshape(own_channels, cell_count)
    block_rows = lax.all_gather(act_padded, "af", axis=0, tiled=True)
    count_rows = block_rows.shape[0]
    products = []
    for offset in tap_offsets:
        backward = (-offset[0], -offset[1], -offset[2])
        shifted = tap_cells(block_rows, backward, planes, height, across).reshape(
            count_rows, cell_count
        )
        products.append(
            lax.dot_general(shifted, flat_grad, contract_last, preferred_element_type=jnp.float32)
        )
    filters = jnp.stack(products, axis=1)
    summed_filters = lax.psum_scatter(filters, "gz", scatter_dimension=0, tiled=True)
    filter_grad = jnp.transpose(summed_filters, (1, 0, 2))
    weight_rows = jnp.transpose(weight, (2, 1, 0)).reshape(channels, 27 * own_channels)
    data_grad = lax.psum_scatter(
        jnp.dot(weight_rows, stacked, preferred_element_type=jnp.float32),
        "af",
        scatter_dimension=0,
        tiled=True,
    )
    return (data_grad.reshape(own_channels, planes, height, across), filter_grad)


def body(inputs, pre_acts, out_grad, weight_one, weight_two):
    pre_float = pre_acts.astype(jnp.float32)
    activation = jnp.where(pre_float > 0, pre_float, 0.3 * pre_float).astype(jnp.bfloat16)
    upper_input, grad_two = layer_back(activation, out_grad, weight_two)
    slopes = jnp.where(pre_float > 0, jnp.float32(1.0), jnp.float32(0.3))
    mid_grad = (upper_input * slopes).astype(jnp.bfloat16)
    lower_input, grad_one = layer_back(inputs, mid_grad, weight_one)
    return (lower_input.astype(jnp.bfloat16), grad_one, grad_two)


def solution(mesh):
    in_specs = (
        P("af", "gz", None, None),
        P("af", "gz", None, None),
        P("af", "gz", None, None),
        P("af", None, None),
        P("af", None, None),
    )
    out_specs = (P("af", "gz", None, None), P(None, "gz", "af"), P(None, "gz", "af"))
    return jax.shard_map(body, mesh=mesh, in_specs=in_specs, out_specs=out_specs, check_vma=False)
```

profile of v0, /device:TPU:8, one launch (start us, length us, event | category | flops | bytes accessed | tf_op | source)
XLA Modules:
  0.0 1131.7 jit_solution(18222383728413994609)
XLA Ops:
  7.2 4.4 collective-permute-start
  11.7 1.3 collective-permute-start.1
  13.0 0.9 collective-permute-done
  13.9 4.5 collective-permute-done.1
  18.4 1.4 select_maximum_fusion
  22.0 0.8 fusion.9
  22.8 1.3 copy.157
  24.2 4.3 collective-permute-start.4
  28.5 1.3 collective-permute-start.5
  29.8 0.6 collective-permute-done.4
  30.4 5.8 collective-permute-done.5
  36.2 1.0 select_maximum_fusion.4
  37.3 31.7 %reduce-scatter.13.cloned.1.call-done = f32[32,1024]{1,0:T(8,128)} async-done(((f32[256,1024]{1,0:T(8,128)}), f32[32,1024]{1,0:T(8,128)}) %reduce-scatter.13.cloned.1.call-update) | async-done | bytes 131088
  69.0 1.1 copy.158
  70.3 2.9 collective-permute-start.2
  73.2 1.3 collective-permute-start.3
  74.5 4.5 collective-permute-start.6
  79.1 1.3 collective-permute-start.7
  81.0 4.3 collective-permute-done.7
  85.2 1.0 select_maximum_fusion.2
  87.8 0.7 copy.119
  88.8 0.8 fusion.12
  89.6 1.4 copy.159
  91.2 34.7 %all-gather.3.cloned.1.call-done = bf16[256,3,10,130]{3,0,2,1:T(8,128)(2,1)} async-done(((bf16[32,3,10,130]{3,0,2,1:T(8,128)(2,1)}), bf16[256,3,10,130]{3,0,2,1:T(8,128)(2,1)}) %all-gather.3.cloned.1.call-update) | async-done | bytes 1996816 | tf_op jit(solution)/shard_map/all_gather | solution.py:51
  126.0 1.4 fusion.68
  127.4 1.6 fusion.67
  129.0 1.6 fusion.66
  130.6 1.3 fusion.65
  131.9 1.6 fusion.64
  133.5 1.6 fusion.63
  135.3 0.4 fusion.61
  136.3 0.4 fusion.58
  137.2 0.4 fusion.55
  138.2 0.4 fusion.52
  139.2 0.4 fusion.49
  140.2 0.4 fusion.46
  141.1 0.4 fusion.43
  141.9 4.4 copy.123
  146.5 32.2 %all-gather.5.cloned.1.call-done = bf16[256,3,10,130]{3,0,2,1:T(8,128)(2,1)} async-done(((bf16[32,3,10,130]{3,0,2,1:T(8,128)(2,1)}), bf16[256,3,10,130]{3,0,2,1:T(8,128)(2,1)}) %all-gather.5.cloned.1.call-update) | async-done | bytes 1996816 | tf_op jit(solution)/shard_map/all_gather | solution.py:51
  178.7 1.4 fusion.41
  180.1 1.6 fusion.40
  181.7 1.6 fusion.39
  183.3 1.3 fusion.38
  184.6 1.6 fusion.37
  186.2 1.6 fusion.36
  188.0 0.4 fusion.34
  188.4 0.3 fusion.33
  189.0 0.4 fusion.31
  190.0 0.4 fusion.28
  190.3 0.3 fusion.27
  190.9 0.4 fusion.25
  191.9 0.4 fusion.22
  192.3 0.3 fusion.21
  192.9 0.4 fusion.19
  193.9 0.4 fusion.16
  194.2 0.3 fusion.15
  194.6 4.4 copy.151
  199.0 22.4 %reduce-scatter.15.cloned.1.call-done = f32[32,1024]{1,0:T(8,128)} async-done(((f32[256,1024]{1,0:T(8,128)}), f32[32,1024]{1,0:T(8,128)}) %reduce-scatter.15.cloned.1.call-update) | async-done | bytes 131088
  221.5 1.1 copy.160
  222.5 0.8 copy.152
  223.3 454.8 %reduce-scatter.9.cloned.1.call-done = f32[4,27,32]{2,1,0:T(8,128)} async-done(((f32[256,27,32]{2,1,0:T(8,128)}), f32[4,27,32]{2,1,0:T(8,128)}) %reduce-scatter.9.cloned.1.call-update) | async-done | bytes 13840 | tf_op jit(solution)/shard_map/reduce_scatter | solution.py:63
  678.1 1.5 copy.153
  679.6 443.8 %reduce-scatter.11.cloned.1.call-done = f32[4,27,32]{2,1,0:T(8,128)} async-done(((f32[256,27,32]{2,1,0:T(8,128)}), f32[4,27,32]{2,1,0:T(8,128)}) %reduce-scatter.11.cloned.1.call-update) | async-done | bytes 13840 | tf_op jit(solution)/shard_map/reduce_scatter | solution.py:63
  1123.4 1.5 copy.154
  (111 shorter events, 12.4 us)
Async XLA Ops:
  7.2 14.8 %copy-start = (bf16[32,27,256]{2,0,1:T(8,128)(2,1)S(1)}, bf16[32,27,256]{2,0,1:T(8,128)(2,1)}, u32[]{:S(2)}) copy-start(bf16[32,27,256]{2,0,1:T(8,128)(2,1)} %param.9) | copy-start | bytes 1327108
  7.2 13.8 %copy-start.1 = (bf16[32,1,8,128]{3,2,1,0:T(8,128)(2,1)S(1)}, bf16[32,1,8,128]{3,2,1,0:T(8,128)(2,1)}, u32[]{:S(2)}) copy-start(bf16[32,1,8,128]{3,2,1,0:T(8,128)(2,1)} %param.7) | copy-start | bytes 196612
  7.2 61.8 %reduce-scatter.13.cloned.1.call-start = ((), (), s32[]{:S(2)}) async-start(), calls=%async_computation.8 | async-start | bytes 1179648
  7.2 6.6 collective-permute-start
  11.7 6.7 collective-permute-start.1
  22.8 1.4 copy-start.3
  24.1 46.2 %copy-start.2 = (bf16[32,1,8,128]{3,2,1,0:T(8,128)(2,1)S(1)}, bf16[32,1,8,128]{3,2,1,0:T(8,128)(2,1)}, u32[]{:S(2)}) copy-start(bf16[32,1,8,128]{3,2,1,0:T(8,128)(2,1)} %param.6) | copy-start | bytes 196612
  24.1 101.9 %all-gather.3.cloned.1.call-start = ((), (), s32[]{:S(2)}) async-start(), calls=%async_computation.4 | async-start | bytes 4423680 | tf_op jit(solution)/shard_map/all_gather | solution.py:51
  24.2 6.2 collective-permute-start.4
  28.5 7.7 collective-permute-start.5
  37.2 141.5 %all-gather.5.cloned.1.call-start = ((), (), s32[]{:S(2)}) async-start(), calls=%async_computation.6 | async-start | bytes 4423680 | tf_op jit(solution)/shard_map/all_gather | solution.py:51
  70.3 10.1 collective-permute-start.2
  73.2 7.2 collective-permute-start.3
  74.5 6.4 collective-permute-start.6
  79.1 6.2 collective-permute-start.7
  86.7 134.7 %reduce-scatter.15.cloned.1.call-start = ((), (), s32[]{:S(2)}) async-start(), calls=%async_computation.9 | async-start | bytes 1179648
  87.8 1.0 copy-start.6
  91.0 587.1 %reduce-scatter.9.cloned.1.call-start = ((), (), s32[]{:S(2)}) async-start(), calls=%async_computation.5 | async-start | bytes 4259840 | tf_op jit(solution)/shard_map/reduce_scatter | solution.py:63
  126.0 9.1 copy-start.4
  146.3 977.1 %reduce-scatter.11.cloned.1.call-start = ((), (), s32[]{:S(2)}) async-start(), calls=%async_computation.7 | async-start | bytes 4259840 | tf_op jit(solution)/shard_map/reduce_scatter | solution.py:63
  178.7 9.1 copy-start.5
Sparse Core Ops, SparseCore 0:
  24.2 44.7 reduce-scatter.12
  71.1 54.8 all-gather.2
  128.1 50.5 all-gather.4
  181.4 40.0 reduce-scatter.14
  224.1 453.9 reduce-scatter.8
  681.0 442.3 reduce-scatter.10
where the time goes:
time: 1130 us
  waiting for transfers between devices  1040 us (92%)
  matrix products  33 us (3%)
  local copies, waits for them, and re-layouts  22.5 us (2%)
  starting transfers between devices  22 us (2%)
  between operations  14.7 us (1%)
    reduce_scatter x2, waiting for transfers between devices, layer_back(): lax.psum_scatter(filters, 'gz', scatter_dimension=0, tiled=True)  899 us
    all_gather x2, waiting for transfers between devices, layer_back(): block_rows = lax.all_gather(act_padded, 'af', axis=0, tiled=True)  66.9 us
    unnamed x8, waiting for transfers between devices  54.2 us
    dot_general x54, matrix products, layer_back(): lax.dot_general(shifted, flat_grad, contract_last, preferred_element_type...  31.5 us
  transfers between devices with their start and end apart: 14, of which 11 were waited for; matrix products, arithmetic and copies ran while one was open for 5% of the time, Pallas kernels for 0%

commit v1 on v0

v1 whole, which is shorter than its diff:
```python
import functools

import jax
import jax.numpy as jnp
from jax import lax
from jax.experimental import pallas as pl
from jax.experimental.pallas import tpu as pltpu
from jax.sharding import PartitionSpec as P

MESH = pl.DeviceIdType.MESH
BF = jnp.bfloat16
F32 = jnp.float32
ZRUN = 8
XRUN = 4
CUT = 384
TAPS = 27
ACROSS = 128
last_dims = (((1,), (1,)), ((), ()))


def kernel(
    slabs, groups, own, height, cut,
    in_hbm, pre_hbm, og_hbm, w1_hbm, w2_hbm,
    ig_ref, f1_ref, f2_ref,
    in_ref, pre_ref, og_ref, w1_ref, w2_ref,
    rel, slope, field, G, WT, U, UP, PS, PR, SB, SR,
    KF, KS, KR, QS, QR,
    XF0, XS0, XR0, ZS0, ZR0, HS0, HR0,
    XF1, XS1, XR1, ZS1, ZR1, HS1, HR1,
    load_s, halo_s, halo_r, ag_s, ag_r, px_s, px_r, y_s, y_r, k_s, k_r, q_s, q_r,
    xs, xr, zs, zr, hs, hr,
):
    cells = height * ACROSS
    chips = groups // 2
    runs = slabs // ZRUN
    halves = runs // XRUN
    rows = groups * own
    share = rows // slabs
    k = lax.axis_index("gz")
    me = lax.axis_index("af")
    chip, core = me // 2, me % 2
    run, z = k // ZRUN, k % ZRUN
    hi, xi = run // XRUN, run % XRUN
    sibling = {"af": chip * 2 + (1 - core)}
    chip_at = lambda d: {"af": lax.rem(chip + d, chips) * 2 + core}
    z_at = lambda d: {"gz": run * ZRUN + lax.rem(z + d, ZRUN)}
    run_at = lambda d: {"gz": lax.rem(run + d, runs) * ZRUN + z}
    x_at = lambda d: {"gz": (hi * XRUN + lax.rem(xi + d, XRUN)) * ZRUN + z}
    hi_at = lambda d: {"gz": (lax.rem(hi + d, halves) * XRUN + xi) * ZRUN + z}
    above = {"gz": lax.rem(k + 1, slabs)}
    below = {"gz": lax.rem(k + slabs - 1, slabs)}
    filled = TAPS * own
    wide = G.shape[0]
    inner = slice(ACROSS, ACROSS + cells)
    columns = ((0, wide), (cut, wide))
    xbufs = ((XF0, XS0, XR0, ZS0, ZR0, HS0, HR0), (XF1, XS1, XR1, ZS1, ZR1, HS1, HR1))

    peers = [sibling, above, below]
    peers += [chip_at(d) for d in range(1, chips)]
    peers += [z_at(d) for d in range(1, ZRUN)]
    peers += [run_at(d) for d in range(1, runs)]
    barrier = pltpu.get_barrier_semaphore()
    for peer in peers:
        pl.semaphore_signal(barrier, inc=1, device_id=peer, device_id_type=MESH)

    loads = []
    for i, (src, dst) in enumerate(
        ((og_hbm, og_ref), (pre_hbm, pre_ref), (w2_hbm, w2_ref), (in_hbm, in_ref), (w1_hbm, w1_ref))
    ):
        loads.append(pltpu.make_async_copy(src, dst, load_s.at[i]))
        loads[-1].start()

    started = []

    def remote(src, dst, s, r, to):
        return pltpu.make_async_remote_copy(
            src_ref=src, dst_ref=dst, send_sem=s, recv_sem=r, device_id=to, device_id_type=MESH
        )

    def send(src, dst, s, r, to):
        copy = remote(src, dst, s, r, to)
        copy.start()
        started.append(copy)
        return copy

    def planes_of(ref):
        rel[...] = ref[...].astype(F32).reshape(own * height, ACROSS)
        return [rel[pl.ds(x, own, stride=height), :] for x in range(height)]

    def at_x(x):
        return slice(x * ACROSS, (x + 1) * ACROSS)

    def halo_copies(l):
        up = remote(field.at[l, 1], field.at[l, 0], halo_s.at[l, 0], halo_r.at[l, 0], above)
        down = remote(field.at[l, 1], field.at[l, 2], halo_s.at[l, 1], halo_r.at[l, 1], below)
        return up, down

    def halo_send(l):
        up, down = halo_copies(l)
        pl.when(k < slabs - 1)(up.start)
        pl.when(k > 0)(down.start)

    def halo_wait(l):
        up, down = halo_copies(l)
        pl.when(k > 0)(up.wait_recv)
        pl.when(k < slabs - 1)(down.wait_recv)

    def halo_done(l):
        up, down = halo_copies(l)
        pl.when(k < slabs - 1)(up.wait_send)
        pl.when(k > 0)(down.wait_send)

    def gather_start(l):
        mine = U.at[l, me]
        found = [
            send(mine, mine, ag_s.at[l, d], ag_r.at[l, d], chip_at(d)) for d in range(1, chips)
        ]
        found.append(send(mine, mine, ag_s.at[l, 0], ag_r.at[l, 0], sibling))
        return found

    def gather_forward(l, found):
        onward = [found[-1]]
        for d in range(1, chips):
            found[d - 1].wait_recv()
            block = U.at[l, lax.rem(chip + chips - d, chips) * 2 + core]
            onward.append(
                send(block, block, ag_s.at[l, chips - 1 + d], ag_r.at[l, chips - 1 + d], sibling)
            )
        return onward

    def gather_finish(onward):
        for copy in onward:
            copy.wait_recv()

    def reorder(l):
        low, mid, top = share.bit_length() - 1, runs.bit_length() - 1, ZRUN.bit_length() - 1
        to_row = lax.broadcasted_iota(jnp.int32, (rows, rows), 0)
        from_row = lax.broadcasted_iota(jnp.int32, (rows, rows), 1)
        wanted = (
            (((to_row >> low) & (runs - 1)) << (low + top))
            | ((to_row >> (low + mid)) << low)
            | (to_row & (share - 1))
        )
        move = jnp.where(from_row == wanted, 1.0, 0.0).astype(BF)
        for n in range(0, cells, 256):
            block = U[l, :, :, n : n + 256].reshape(rows, 256)
            UP[:, n : n + 256] = jnp.dot(move, block, preferred_element_type=F32).astype(BF)

    def turn(l, w_ref):
        full = jnp.concatenate([w_ref[...], jnp.zeros((wide - filled, rows), BF)], axis=0).T
        for g in range(groups):
            WT[l, g % 2, (g // 2) * own : (g // 2 + 1) * own, :] = full[g * own : (g + 1) * own, :]

    lane = lax.broadcasted_iota(jnp.int32, (own, ACROSS), 1)
    number = lambda a, b, c: 9 * (a + 1) + 3 * (b + 1) + (c + 1)
    tap_rows = lambda t: slice(t * own, (t + 1) * own)

    def build(l, p):
        a = 1 - p

        def step(x, carry):
            v = field[l, p, :, pl.ds(pl.multiple_of(x * ACROSS, ACROSS), ACROSS)].astype(F32)
            for c in (-1, 0, 1):
                if c == 0:
                    s = v
                else:
                    edge = 0 if c == 1 else ACROSS - 1
                    s = jnp.where(lane == edge, 0.0, pltpu.roll(v, c % ACROSS, 1))
                s = s.astype(BF)
                for b in (-1, 0, 1):
                    at = pl.ds(pl.multiple_of((x + b + 1) * ACROSS, ACROSS), ACROSS)
                    G[tap_rows(number(a, b, c)), at] = s
            return carry

        lax.fori_loop(0, height, step, 0)

    def grad_product(l, half, which):
        for n in range(0, cells, 256):
            PS[l, half, :, n : n + 256] = jnp.dot(
                WT[l, which], G[:, ACROSS + n : ACROSS + n + 256], preferred_element_type=F32
            )

    def grad_first(l):
        grad_product(l, 0, 1 - core)
        copy = send(PS.at[l, 0], PR.at[l], px_s.at[l], px_r.at[l], sibling)
        grad_product(l, 1, core)
        return copy

    def grad_second(l, copy):
        copy.wait_recv()
        for j in range(chips):
            at = slice(j * own, (j + 1) * own)
            total = PS[l, 1, at, :] + PR[l, at, :]
            PS[l, 1, at, :] = total
            SB[l, j] = total.astype(BF)
        return [
            send(
                SB.at[l, lax.rem(chip + d, chips)], SR.at[l, d - 1],
                y_s.at[l, d - 1], y_r.at[l, d - 1], chip_at(d),
            )
            for d in range(1, chips)
        ]

    def grad_last(l, copies):
        for copy in copies:
            copy.wait_recv()
        mine = pl.ds(pl.multiple_of(chip * own, own), own)

        def at(x):
            total = PS[l, 1, mine, at_x(x)]
            for d in range(chips - 1):
                total = total + SR[l, d, :, at_x(x)].astype(F32)
            return total

        return at

    def z_first():
        for n in range(0, cut, 256):
            size = min(256, cut - n)
            block = lax.dot_general(
                UP[...], G[n : n + size, inner], last_dims, preferred_element_type=F32
            ).reshape(ZRUN, runs * share, size)
            KF[:, :, n : n + size] = block
            KS[:, :, n : n + size] = block.astype(BF)
        return [
            send(KS.at[lax.rem(z + d, ZRUN)], KR.at[d - 1], k_s.at[d - 1], k_r.at[d - 1], z_at(d))
            for d in range(1, ZRUN)
        ]

    def z_first_then(copies):
        for copy in copies:
            copy.wait_recv()
        for n in range(0, cut, 128):
            at = slice(n, n + 128)
            total = KF[z, :, at]
            for d in range(ZRUN - 1):
                total = total + KR[d, :, at].astype(F32)
            for j in range(runs):
                QS[j, :, at] = total[j * share : (j + 1) * share, :]
        return [
            send(QS.at[lax.rem(run + d, runs)], QR.at[d - 1], q_s.at[d - 1], q_r.at[d - 1], run_at(d))
            for d in range(1, runs)
        ]

    def z_first_last(copies, out_ref):
        for copy in copies:
            copy.wait_recv()
        total = QS[run]
        for d in range(runs - 1):
            total = total + QR[d]
        out_ref[:, :cut] = total

    def x_first(l):
        start, stop = columns[l]
        XF, XS, XR = xbufs[l][:3]
        for n in range(start, stop, 256):
            size = min(256, stop - n)
            at = slice(n - start, n - start + size)
            block = lax.dot_general(
                U[l].reshape(rows, cells), G[n : n + size, inner], last_dims,
                preferred_element_type=F32,
            )
            for h in range(halves):
                for x in range(XRUN):
                    j = (h * XRUN + x) * ZRUN * share
                    part = block[j : j + ZRUN * share, :]
                    XF[x, h, :, at] = part
                    XS[x, h, :, at] = part.astype(BF)
        return [
            send(
                XS.at[lax.rem(xi + d, XRUN)], XR.at[d - 1],
                xs.at[l, d - 1], xr.at[l, d - 1], x_at(d),
            )
            for d in range(1, XRUN)
        ]

    def x_first_then(l, copies):
        start, stop = columns[l]
        XF, XS, XR, ZS, ZR = xbufs[l][:5]
        for copy in copies:
            copy.wait_recv()
        for n in range(0, stop - start, 128):
            at = slice(n, n + 128)
            for h in range(halves):
                total = XF[xi, h, :, at]
                for d in range(XRUN - 1):
                    total = total + XR[d, h, :, at].astype(F32)
                for j in range(ZRUN):
                    ZS[j, h * share : (h + 1) * share, at] = total[j * share : (j + 1) * share, :]
        return [
            send(
                ZS.at[lax.rem(z + d, ZRUN)], ZR.at[d - 1],
                zs.at[l, d - 1], zr.at[l, d - 1], z_at(d),
            )
            for d in range(1, ZRUN)
        ]

    def x_first_pair(l, copies):
        ZS, ZR, HS, HR = xbufs[l][3:]
        for copy in copies:
            copy.wait_recv()
        total = ZS[z]
        for d in range(ZRUN - 1):
            total = total + ZR[d]
        for h in range(halves):
            HS[h] = total[h * share : (h + 1) * share, :]
        return [
            send(
                HS.at[lax.rem(hi + d, halves)], HR.at[d - 1],
                hs.at[l, d - 1], hr.at[l, d - 1], hi_at(d),
            )
            for d in range(1, halves)
        ]

    def x_first_last(l, copies, out_ref):
        start, stop = columns[l]
        HS, HR = xbufs[l][5:]
        for copy in copies:
            copy.wait_recv()
        total = HS[hi]
        for d in range(halves - 1):
            total = total + HR[d]
        out_ref[:, start:stop] = total

    loads[0].wait()
    for x, v in enumerate(planes_of(og_ref)):
        field[0, 1, :, at_x(x)] = v.astype(BF)
    loads[1].wait()
    for x, v in enumerate(planes_of(pre_ref)):
        slope[:, at_x(x)] = jnp.where(v > 0, jnp.float32(1.0), jnp.float32(0.3))
        U[0, me, :, at_x(x)] = jnp.where(v > 0, v, 0.3 * v).astype(BF)

    @pl.when(k == 0)
    def _():
        for l in range(2):
            field[l, 0] = jnp.zeros((own, cells), BF)

    @pl.when(k == slabs - 1)
    def _():
        for l in range(2):
            field[l, 2] = jnp.zeros((own, cells), BF)

    pl.semaphore_wait(barrier, len(peers))
    halo_send(0)
    gather_act = gather_start(0)

    none = jnp.zeros((own, ACROSS), BF)
    for a in (-1, 0, 1):
        for c in (-1, 0, 1):
            G[tap_rows(number(a, 1, c)), at_x(1)] = none
            G[tap_rows(number(a, -1, c)), at_x(height)] = none
    if wide > filled:
        G[filled:, :] = jnp.zeros((wide - filled, G.shape[1]), BF)

    build(0, 1)
    loads[2].wait()
    turn(0, w2_ref)
    halo_wait(0)
    build(0, 0)
    build(0, 2)
    pair = grad_first(0)
    loads[3].wait()
    for x, v in enumerate(planes_of(in_ref)):
        U[1, me, :, at_x(x)] = v.astype(BF)
    parts = grad_second(0, pair)
    loads[4].wait()
    turn(1, w1_ref)
    onward = gather_forward(0, gather_act)
    gather_finish(onward)
    two = x_first(0)
    total_at = grad_last(0, parts)
    for x in range(height):
        field[1, 1, :, at_x(x)] = (total_at(x) * slope[:, at_x(x)]).astype(BF)
    halo_send(1)
    gather_in = gather_start(1)
    build(1, 1)
    halo_wait(1)
    build(1, 0)
    build(1, 2)
    pair = grad_first(1)
    parts = grad_second(1, pair)
    two = x_first_then(0, two)
    onward = gather_forward(1, gather_in)
    gather_finish(onward)
    reorder(1)
    one_z = z_first()
    one_x = x_first(1)
    two = x_first_pair(0, two)
    total_at = grad_last(1, parts)
    for x in range(height):
        rel[pl.ds(x, own, stride=height), :] = total_at(x)
    ig_ref[...] = rel[...].reshape(own, height, ACROSS).astype(BF)
    one_x = x_first_then(1, one_x)
    one_z = z_first_then(one_z)
    x_first_last(0, two, f2_ref)
    one_x = x_first_pair(1, one_x)
    z_first_last(one_z, f1_ref)
    x_first_last(1, one_x, f1_ref)
    halo_done(0)
    halo_done(1)
    for copy in started:
        copy.wait_send()


def body(slabs, groups, inputs, pre_acts, out_grad, weight_one, weight_two):
    own, planes, height, across = out_grad.shape
    channels = weight_one.shape[2]
    cells = height * across
    chips = groups // 2
    runs = slabs // ZRUN
    halves = runs // XRUN
    share = channels // slabs
    wide = -(-TAPS * own // 128) * 128
    cut = CUT
    flat = lambda v: v.reshape(own, height, across)
    taps = lambda w: jnp.transpose(w, (1, 0, 2)).reshape(TAPS * own, channels)
    vmem = pl.BlockSpec(memory_space=pltpu.VMEM)
    hbm = pl.BlockSpec(memory_space=pltpu.HBM)
    scratch = [pltpu.VMEM((own, height, across), BF)] * 3
    scratch += [pltpu.VMEM((TAPS * own, channels), BF)] * 2
    scratch += [
        pltpu.VMEM((own * height, across), F32),
        pltpu.VMEM((own, cells), F32),
        pltpu.VMEM((2, 3, own, cells), BF),
        pltpu.VMEM((wide, cells + 2 * across), BF),
        pltpu.VMEM((2, 2, chips * own, wide), BF),
        pltpu.VMEM((2, groups, own, cells), BF),
        pltpu.VMEM((channels, cells), BF),
        pltpu.VMEM((2, 2, chips * own, cells), F32),
        pltpu.VMEM((2, chips * own, cells), F32),
        pltpu.VMEM((2, chips, own, cells), BF),
        pltpu.VMEM((2, chips - 1, own, cells), BF),
        pltpu.VMEM((ZRUN, runs * share, cut), F32),
        pltpu.VMEM((ZRUN, runs * share, cut), BF),
        pltpu.VMEM((ZRUN - 1, runs * share, cut), BF),
        pltpu.VMEM((runs, share, cut), F32),
        pltpu.VMEM((runs - 1, share, cut), F32),
    ]
    for width in (wide, wide - cut):
        scratch += [
            pltpu.VMEM((XRUN, halves, ZRUN * share, width), F32),
            pltpu.VMEM((XRUN, halves, ZRUN * share, width), BF),
            pltpu.VMEM((XRUN - 1, halves, ZRUN * share, width), BF),
            pltpu.VMEM((ZRUN, halves * share, width), F32),
            pltpu.VMEM((ZRUN - 1, halves * share, width), F32),
            pltpu.VMEM((halves, share, width), F32),
            pltpu.VMEM((halves - 1, share, width), F32),
        ]
    scratch.append(pltpu.SemaphoreType.DMA((5,)))
    for shape in (
        (2, 2), (2, 2 * chips - 1), (2,), (2, chips - 1), (ZRUN - 1,), (runs - 1,),
        (2, XRUN - 1), (2, ZRUN - 1), (2, halves - 1),
    ):
        scratch += [pltpu.SemaphoreType.DMA(shape), pltpu.SemaphoreType.DMA(shape)]
    input_grad, one, two = pl.pallas_call(
        functools.partial(kernel, slabs, groups, own, height, cut),
        out_shape=[
            jax.ShapeDtypeStruct((own, height, across), BF),
            jax.ShapeDtypeStruct((share, wide), F32),
            jax.ShapeDtypeStruct((share, wide), F32),
        ],
        in_specs=[hbm] * 5,
        out_specs=[vmem] * 3,
        scratch_shapes=scratch,
        compiler_params=pltpu.CompilerParams(
            collective_id=0, has_side_effects=True, vmem_limit_bytes=60 * 1024 * 1024
        ),
        name="conv_back",
    )(flat(inputs), flat(pre_acts), flat(out_grad), taps(weight_one), taps(weight_two))

    def filters(v):
        return jnp.transpose(v[:, : TAPS * own].reshape(share, TAPS, own), (1, 0, 2))

    return input_grad.reshape(own, planes, height, across), filters(one), filters(two)


def solution(mesh):
    in_specs = (
        P("af", "gz", None, None),
        P("af", "gz", None, None),
        P("af", "gz", None, None),
        P("af", None, None),
        P("af", None, None),
    )
    out_specs = (P("af", "gz", None, None), P(None, "gz", "af"), P(None, "gz", "af"))
    return jax.shard_map(
        functools.partial(body, mesh.shape["gz"], mesh.shape["af"]),
        mesh=mesh, in_specs=in_specs, out_specs=out_specs, check_vma=False,
    )
```

time: 1130 us -> 72 us (0.06)
  waiting for transfers between devices: 1040 us -> 0 us
  Pallas kernels: 0 us -> 68 us
  matrix products: 33 us -> 0 us
  starting transfers between devices: 22 us -> 0 us
  local copies, waits for them, and re-layouts: 22.5 us -> 3.05 us
  between operations: 14.7 us -> 0.66 us
    reduce_scatter x2 -> x0, waiting for transfers between devices: 899 us -> none  [layer_back(): lax.psum_scatter(filters, 'gz', scatter_dimension=0, tiled=True)]
    pallas_call x0 -> x1, Pallas kernels: none -> 68 us  [body(): pl.pallas_call(functools.partial(kernel, slabs, groups, own, height, cut)...]
    all_gather x2 -> x0, waiting for transfers between devices: 66.9 us -> none  [layer_back(): block_rows = lax.all_gather(act_padded, 'af', axis=0, tiled=True)]
    unnamed x8 -> x0, waiting for transfers between devices: 54.2 us -> none
    dot_general x56 -> x0, matrix products: 33 us -> none  [the longest x54 31.5 us: layer_back(): lax.dot_general(shifted, flat_grad, contract_last, preferred_element_type...]
    ppermute x8 -> x0, starting transfers between devices: 21.3 us -> none  [the longest x4 16.1 us: with_halo(): lax.ppermute(tail, axis, [(i, (i + 1) % count) for i in range(ends)])]
    ppermute x8 -> x0, waiting for transfers between devices: 16.1 us -> none  [the longest x4 14.6 us: with_halo(): lax.ppermute(head, axis, [((i + 1) % count, i) for i in range(ends)])]
  transfers between devices with their start and end apart: 14 -> 0, of which waited for: 11 -> 0; matrix products, arithmetic and copies ran while one was open for 5% -> 0% of each run, Pallas kernels for 0% -> 0%
where the time goes in v1:
time: 72 us; the launch traced here: 71.7 us
  Pallas kernels  68 us (94%)
  local copies, waits for them, and re-layouts  3.05 us (4%)
    pallas_call x1, Pallas kernels, body(): pl.pallas_call(functools.partial(kernel, slabs, groups, own, height, cut)...  68 us
    unnamed x7, local copies, waits for them, and re-layouts  2.17 us

profile of v1, /device:TPU:8, one launch (start us, length us, event | category | flops | bytes accessed | tf_op | source)
XLA Modules:
  0.0 71.7 jit_solution(8486249213180350654)
XLA Ops:
  0.6 68.0 %conv_back.1 = (bf16[32,8,128]{2,1,0:T(8,128)(2,1)}, f32[4,896]{1,0:T(4,128)}, f32[4,896]{1,0:T(4,128)}) custom-call(bf16[32,8,128]{2,1,0:T(8,128)(2,1)} %bitcast.20, bf16[32,8,128]{2,1,0:T(8,128)(2,1)} %bitcast.21, bf16[32,8,128]{2,1,0:T(8,128)(2,1)} %bitcast.22, bf16[864,256]{1,0:T(8,128)(2,1)} %bitcast.16, bf16[864,256]{1,0:T(8,128)(2,1)} %bitcast.17), custom_call_target="tpu_custom_call" | custom-call | tf_op jit(solution)/shard_map/conv_back/pallas_call | solution.py:455
  68.6 0.8 %reshape.36 = f32[4,27,32]{2,1,0:T(8,128)S(1)} reshape(f32[4,864]{1,0:T(4,128)} %bitcast.25) | data formatting | bytes 27648 | tf_op jit(solution)/shard_map/reshape | solution.py:472
  69.5 0.0 copy-start.1
  69.5 0.7 copy.12
  70.1 0.0 copy-done.1
  70.2 0.1 reshape.37
  70.3 0.0 copy-start
  70.3 0.7 copy.13
  70.9 0.2 copy-done
  71.1 0.6 copy.15
Async XLA Ops:
  69.5 0.7 copy-start.1
  70.3 0.8 %copy-start = (bf16[32,8,128]{2,1,0:T(8,128)(2,1)S(1)}, bf16[32,8,128]{2,1,0:T(8,128)(2,1)}, u32[]{:S(2)}) copy-start(bf16[32,8,128]{2,1,0:T(8,128)(2,1)} %get-tuple-element.6) | copy-start | bytes 196612

commit v2 on v1

v2 whole, which is shorter than its diff:
```python
import functools

import jax
import jax.numpy as jnp
from jax import lax
from jax.experimental import pallas as pl
from jax.experimental.pallas import tpu as pltpu
from jax.sharding import PartitionSpec as P

MESH = pl.DeviceIdType.MESH
BF = jnp.bfloat16
F32 = jnp.float32
ZRUN = 8
XRUN = 4
CUTS = (256, 512)
PIECES = 4
ORDER = (0, -1, 1)
TAPS = 27
ACROSS = 128
last_dims = (((1,), (1,)), ((), ()))


def kernel(
    slabs, groups, own, height, cuts,
    in_hbm, pre_hbm, og_hbm, w1_hbm, w2_hbm,
    ig_ref, f1_ref, f2_ref,
    in_ref, pre_ref, og_ref, w1_ref, w2_ref,
    rel, slope, field, G, WT, U, UP, PS, PR, SB, SR,
    KF0, KS0, KR0, QS0, QR0,
    KF1, KS1, KR1, QS1, QR1,
    XF0, XS0, XR0, ZF0, ZS0, ZR0, HS0, HR0,
    XF1, XS1, XR1, ZF1, ZS1, ZR1, HS1, HR1,
    load_s, halo_s, halo_r, ag_s, ag_r, px_s, px_r, y_s, y_r, k_s, k_r, q_s, q_r,
    xs, xr, zs, zr, hs, hr,
):
    cells = height * ACROSS
    chips = groups // 2
    runs = slabs // ZRUN
    halves = runs // XRUN
    rows = groups * own
    share = rows // slabs
    k = lax.axis_index("gz")
    me = lax.axis_index("af")
    chip, core = me // 2, me % 2
    run, z = k // ZRUN, k % ZRUN
    hi, xi = run // XRUN, run % XRUN
    sibling = {"af": chip * 2 + (1 - core)}
    chip_at = lambda d: {"af": lax.rem(chip + d, chips) * 2 + core}
    z_at = lambda d: {"gz": run * ZRUN + lax.rem(z + d, ZRUN)}
    run_at = lambda d: {"gz": lax.rem(run + d, runs) * ZRUN + z}
    x_at = lambda d: {"gz": (hi * XRUN + lax.rem(xi + d, XRUN)) * ZRUN + z}
    hi_at = lambda d: {"gz": (lax.rem(hi + d, halves) * XRUN + xi) * ZRUN + z}
    above = {"gz": lax.rem(k + 1, slabs)}
    below = {"gz": lax.rem(k + slabs - 1, slabs)}
    filled = TAPS * own
    wide = G.shape[0]
    inner = slice(ACROSS, ACROSS + cells)
    part = cells // PIECES
    step = height // PIECES
    place = k % (ZRUN * XRUN)
    edge = (place == 0) | (place == ZRUN * XRUN - 1)
    crossed = (place == ZRUN - 1) | (place == ZRUN * (XRUN - 1))
    columns = ((0, wide), (cuts[-1], wide))
    zbufs = ((KF0, KS0, KR0, QS0, QR0), (KF1, KS1, KR1, QS1, QR1))
    xbufs = ((XF0, XS0, XR0, ZF0, ZS0, ZR0, HS0, HR0), (XF1, XS1, XR1, ZF1, ZS1, ZR1, HS1, HR1))

    peers = [sibling, above, below]
    peers += [chip_at(d) for d in range(1, chips)]
    peers += [z_at(d) for d in range(1, ZRUN)]
    peers += [run_at(d) for d in range(1, runs)]
    barrier = pltpu.get_barrier_semaphore()
    for peer in peers:
        pl.semaphore_signal(barrier, inc=1, device_id=peer, device_id_type=MESH)

    loads = []
    for i, (src, dst) in enumerate(
        ((og_hbm, og_ref), (pre_hbm, pre_ref), (w2_hbm, w2_ref), (in_hbm, in_ref), (w1_hbm, w1_ref))
    ):
        loads.append(pltpu.make_async_copy(src, dst, load_s.at[i]))
        loads[-1].start()

    started = []

    def remote(src, dst, s, r, to):
        return pltpu.make_async_remote_copy(
            src_ref=src, dst_ref=dst, send_sem=s, recv_sem=r, device_id=to, device_id_type=MESH
        )

    def send(src, dst, s, r, to):
        copy = remote(src, dst, s, r, to)
        copy.start()
        started.append(copy)
        return copy

    def planes_of(ref):
        rel[...] = ref[...].astype(F32).reshape(own * height, ACROSS)
        return [rel[pl.ds(x, own, stride=height), :] for x in range(height)]

    def at_x(x):
        return slice(x * ACROSS, (x + 1) * ACROSS)

    def halo_copies(l, q):
        own_plane, low, high = (field.at[l, p, q] for p in (1, 0, 2))
        up = remote(own_plane, low, halo_s.at[l, q, 0], halo_r.at[l, q, 0], above)
        down = remote(own_plane, high, halo_s.at[l, q, 1], halo_r.at[l, q, 1], below)
        return up, down

    def halo_send(l, q):
        up, down = halo_copies(l, q)
        pl.when(k < slabs - 1)(up.start)
        pl.when(k > 0)(down.start)

    def halo_wait(l, q):
        up, down = halo_copies(l, q)
        pl.when(k > 0)(up.wait_recv)
        pl.when(k < slabs - 1)(down.wait_recv)

    def halo_done(l, q):
        up, down = halo_copies(l, q)
        pl.when(k < slabs - 1)(up.wait_send)
        pl.when(k > 0)(down.wait_send)

    def gather_copies(l):
        mine = U.at[l, me]
        found = [
            remote(mine, mine, ag_s.at[l, d], ag_r.at[l, d], chip_at(d)) for d in range(1, chips)
        ]
        found.append(remote(mine, mine, ag_s.at[l, 0], ag_r.at[l, 0], sibling))
        return found

    def gather_start(l, found, when):
        @pl.when(when)
        def _():
            for copy in found:
                copy.start()

    def gather_forward(l, found):
        started.extend(found)
        onward = [found[-1]]
        for d in range(1, chips):
            found[d - 1].wait_recv()
            block = U.at[l, lax.rem(chip + chips - d, chips) * 2 + core]
            onward.append(
                send(block, block, ag_s.at[l, chips - 1 + d], ag_r.at[l, chips - 1 + d], sibling)
            )
        return onward

    def gather_finish(onward):
        for copy in onward:
            copy.wait_recv()

    def reorder(l):
        low, mid, top = share.bit_length() - 1, runs.bit_length() - 1, ZRUN.bit_length() - 1
        to_row = lax.broadcasted_iota(jnp.int32, (rows, rows), 0)
        from_row = lax.broadcasted_iota(jnp.int32, (rows, rows), 1)
        wanted = (
            (((to_row >> low) & (runs - 1)) << (low + top))
            | ((to_row >> (low + mid)) << low)
            | (to_row & (share - 1))
        )
        move = jnp.where(from_row == wanted, 1.0, 0.0).astype(BF)
        for n in range(0, cells, 256):
            block = U[l, :, :, n : n + 256].reshape(rows, 256)
            UP[:, n : n + 256] = jnp.dot(move, block, preferred_element_type=F32).astype(BF)

    def turn(l, w_ref):
        third = filled // 3
        blocks = [w_ref[(a + 1) * third : (a + 2) * third, :] for a in ORDER]
        full = jnp.concatenate(blocks + [jnp.zeros((wide - filled, rows), BF)], axis=0).T
        for g in range(groups):
            WT[l, g % 2, (g // 2) * own : (g // 2 + 1) * own, :] = full[g * own : (g + 1) * own, :]

    lane = lax.broadcasted_iota(jnp.int32, (own, ACROSS), 1)
    number = lambda a, b, c: 9 * ORDER.index(a) + 3 * (b + 1) + (c + 1)
    tap_rows = lambda t: slice(t * own, (t + 1) * own)

    def build(l, p, q):
        a = 1 - p
        for x in range(q * step, (q + 1) * step):
            v = field[l, p, q, :, at_x(x - q * step)].astype(F32)
            for c in (-1, 0, 1):
                if c == 0:
                    s = v
                else:
                    edge = 0 if c == 1 else ACROSS - 1
                    s = jnp.where(lane == edge, 0.0, pltpu.roll(v, c % ACROSS, 1))
                s = s.astype(BF)
                for b in (-1, 0, 1):
                    if 0 <= x + b < height:
                        G[tap_rows(number(a, b, c)), at_x(x + b + 1)] = s

    def grad_product(l, half, which, q):
        at = slice(ACROSS + q * part, ACROSS + (q + 1) * part)
        PS[l, half, q] = jnp.dot(WT[l, which], G[:, at], preferred_element_type=F32)

    def grad_first(l, q):
        grad_product(l, 0, 1 - core, q)
        copy = send(PS.at[l, 0, q], PR.at[l, q], px_s.at[l, q], px_r.at[l, q], sibling)
        grad_product(l, 1, core, q)
        return copy

    def grad_second(l, q, copy):
        copy.wait_recv()
        for j in range(chips):
            at = slice(j * own, (j + 1) * own)
            total = PS[l, 1, q, at, :] + PR[l, q, at, :]
            PS[l, 1, q, at, :] = total
            SB[l, q, j] = total.astype(BF)
        return [
            send(
                SB.at[l, q, lax.rem(chip + d, chips)], SR.at[l, q, d - 1],
                y_s.at[l, q, d - 1], y_r.at[l, q, d - 1], chip_at(d),
            )
            for d in range(1, chips)
        ]

    def grad_last(l, q, found):
        for copy in found:
            copy.wait_recv()
        mine = pl.ds(pl.multiple_of(chip * own, own), own)
        total = PS[l, 1, q, mine, :]
        for d in range(chips - 1):
            total = total + SR[l, q, d].astype(F32)
        return total

    def by_tap(total, start, out_ref):
        for i in range(total.shape[1] // own):
            block = start // own + i
            if block < TAPS:
                out_ref[9 * (ORDER[block // 9] + 1) + block % 9] = total[:, i * own : (i + 1) * own]

    zcolumns = ((0, cuts[0]), (cuts[0], cuts[1]))

    def z_first(i):
        KF, KS, KR = zbufs[i][:3]
        start, stop = zcolumns[i]
        for n in range(start, stop, 256):
            size = min(256, stop - n)
            at = slice(n - start, n - start + size)
            block = lax.dot_general(
                UP[...], G[n : n + size, inner], last_dims, preferred_element_type=F32
            ).reshape(ZRUN, runs * share, size)
            KF[:, :, at] = block
            KS[:, :, at] = block.astype(BF)
        return [
            send(
                KS.at[lax.rem(z + d, ZRUN)], KR.at[d - 1],
                k_s.at[i, d - 1], k_r.at[i, d - 1], z_at(d),
            )
            for d in range(1, ZRUN)
        ]

    def z_first_then(i, copies):
        KF, KS, KR, QS, QR = zbufs[i]
        for copy in copies:
            copy.wait_recv()
        for n in range(0, KF.shape[2], 128):
            at = slice(n, n + 128)
            total = KF[z, :, at]
            for d in range(ZRUN - 1):
                total = total + KR[d, :, at].astype(F32)
            for j in range(runs):
                QS[j, :, at] = total[j * share : (j + 1) * share, :]
        return [
            send(
                QS.at[lax.rem(run + d, runs)], QR.at[d - 1],
                q_s.at[i, d - 1], q_r.at[i, d - 1], run_at(d),
            )
            for d in range(1, runs)
        ]

    def z_first_last(i, copies, out_ref):
        QS, QR = zbufs[i][3:]
        for copy in copies:
            copy.wait_recv()
        total = QS[run]
        for d in range(runs - 1):
            total = total + QR[d]
        by_tap(total, zcolumns[i][0], out_ref)

    def x_first(l):
        start, stop = columns[l]
        XF, XS, XR = xbufs[l][:3]
        for n in range(start, stop, 256):
            size = min(256, stop - n)
            at = slice(n - start, n - start + size)
            block = lax.dot_general(
                U[l].reshape(rows, cells), G[n : n + size, inner], last_dims,
                preferred_element_type=F32,
            )
            for h in range(halves):
                for x in range(XRUN):
                    j = (h * XRUN + x) * ZRUN * share
                    part = block[j : j + ZRUN * share, :]
                    XF[x, h, :, at] = part
                    XS[x, h, :, at] = part.astype(BF)
        return [
            send(
                XS.at[lax.rem(xi + d, XRUN)], XR.at[d - 1],
                xs.at[l, d - 1], xr.at[l, d - 1], x_at(d),
            )
            for d in range(1, XRUN)
        ]

    def x_first_then(l, copies):
        start, stop = columns[l]
        XF, XS, XR, ZF, ZS, ZR = xbufs[l][:6]
        eight = halves * share
        for copy in copies:
            copy.wait_recv()
        for n in range(0, stop - start, 128):
            at = slice(n, n + 128)
            fold, to = divmod(n, ZS.shape[2])
            to = slice(to, to + 128)
            for h in range(halves):
                total = XF[xi, h, :, at]
                for d in range(XRUN - 1):
                    total = total + XR[d, h, :, at].astype(F32)
                first = fold * eight + h * share
                for j in range(ZRUN):
                    ZF[j, first : first + share, to] = total[j * share : (j + 1) * share, :]
        for j in range(ZRUN):
            ZS[j] = ZF[j].astype(BF)
        return [
            send(
                ZS.at[lax.rem(z + d, ZRUN)], ZR.at[d - 1],
                zs.at[l, d - 1], zr.at[l, d - 1], z_at(d),
            )
            for d in range(1, ZRUN)
        ]

    def x_first_pair(l, copies):
        start, stop = columns[l]
        ZF, ZS, ZR, HS, HR = xbufs[l][3:]
        eight = halves * share
        for copy in copies:
            copy.wait_recv()
        total = ZF[z]
        for d in range(ZRUN - 1):
            total = total + ZR[d].astype(F32)
        fold = total.shape[1]
        for h in range(halves):
            HS[h, :, :fold] = total[h * share : (h + 1) * share, :]
            rest = stop - start - fold
            HS[h, :, fold:] = total[eight + h * share : eight + (h + 1) * share, :rest]
        return [
            send(
                HS.at[lax.rem(hi + d, halves)], HR.at[d - 1],
                hs.at[l, d - 1], hr.at[l, d - 1], hi_at(d),
            )
            for d in range(1, halves)
        ]

    def x_first_last(l, copies, out_ref):
        start, stop = columns[l]
        HS, HR = xbufs[l][6:]
        for copy in copies:
            copy.wait_recv()
        total = HS[hi]
        for d in range(halves - 1):
            total = total + HR[d]
        by_tap(total, start, out_ref)

    loads[0].wait()
    for x, v in enumerate(planes_of(og_ref)):
        field[0, 1, x // step, :, at_x(x % step)] = v.astype(BF)
    loads[1].wait()
    for x, v in enumerate(planes_of(pre_ref)):
        slope[x // step, :, at_x(x % step)] = jnp.where(v > 0, jnp.float32(1.0), jnp.float32(0.3))
        U[0, me, :, at_x(x)] = jnp.where(v > 0, v, 0.3 * v).astype(BF)
    loads[3].wait()
    for x, v in enumerate(planes_of(in_ref)):
        U[1, me, :, at_x(x)] = v.astype(BF)

    @pl.when(k == 0)
    def _():
        for l in range(2):
            field[l, 0] = jnp.zeros(field.shape[2:], BF)

    @pl.when(k == slabs - 1)
    def _():
        for l in range(2):
            field[l, 2] = jnp.zeros(field.shape[2:], BF)

    pl.semaphore_wait(barrier, len(peers))
    for q in range(PIECES):
        halo_send(0, q)
    gather_act, gather_in = gather_copies(0), gather_copies(1)
    gather_start(0, gather_act, jnp.logical_not(crossed))
    gather_start(1, gather_in, edge)

    none = jnp.zeros((own, ACROSS), BF)
    for a in (-1, 0, 1):
        for c in (-1, 0, 1):
            G[tap_rows(number(a, 1, c)), at_x(1)] = none
            G[tap_rows(number(a, -1, c)), at_x(height)] = none
    if wide > filled:
        G[filled:, :] = jnp.zeros((wide - filled, G.shape[1]), BF)

    def grad_pieces(l, last):
        pair, parts = [], []
        for q in range(PIECES):
            halo_wait(l, q)
            build(l, 0, q)
            build(l, 2, q)
            if q > 0:
                pair.append(grad_first(l, q - 1))
            if q > 1:
                parts.append(grad_second(l, q - 2, pair[q - 2]))
        pair.append(grad_first(l, PIECES - 1))
        last()
        for q in range(PIECES - 2, PIECES):
            parts.append(grad_second(l, q, pair[q]))
        return parts

    for q in range(PIECES):
        build(0, 1, q)
    loads[2].wait()
    turn(0, w2_ref)
    parts = grad_pieces(0, lambda: None)
    gather_start(0, gather_act, crossed)
    loads[4].wait()
    turn(1, w1_ref)
    onward = gather_forward(0, gather_act)
    gather_finish(onward)
    two = x_first(0)
    for q in range(PIECES):
        field[1, 1, q] = (grad_last(0, q, parts[q]) * slope[q]).astype(BF)
        halo_send(1, q)
        if q == 0:
            gather_start(1, gather_in, jnp.logical_not(edge))
    for q in range(PIECES):
        build(1, 1, q)
    onward = gather_forward(1, gather_in)
    gather_finish(onward)
    reorder(1)
    one_early = z_first(0)
    two = x_first_then(0, two)
    late = []

    def products():
        late.append(x_first(1))
        late.append(z_first(1))

    parts = grad_pieces(1, products)
    one_x, one_late = late
    two = x_first_pair(0, two)
    one_early = z_first_then(0, one_early)
    one_x = x_first_then(1, one_x)
    one_late = z_first_then(1, one_late)
    x_first_last(0, two, f2_ref)
    z_first_last(0, one_early, f1_ref)
    for q in range(PIECES):
        total = grad_last(1, q, parts[q])
        for x in range(step):
            rel[pl.ds(q * step + x, own, stride=height), :] = total[:, at_x(x)]
    ig_ref[...] = rel[...].reshape(own, height, ACROSS).astype(BF)
    one_x = x_first_pair(1, one_x)
    z_first_last(1, one_late, f1_ref)
    x_first_last(1, one_x, f1_ref)
    for l in range(2):
        for q in range(PIECES):
            halo_done(l, q)
    for copy in started:
        copy.wait_send()


def body(slabs, groups, inputs, pre_acts, out_grad, weight_one, weight_two):
    own, planes, height, across = out_grad.shape
    channels = weight_one.shape[2]
    cells = height * across
    chips = groups // 2
    runs = slabs // ZRUN
    halves = runs // XRUN
    share = channels // slabs
    wide = -(-TAPS * own // 128) * 128
    cuts = CUTS
    flat = lambda v: v.reshape(own, height, across)
    taps = lambda w: jnp.transpose(w, (1, 0, 2)).reshape(TAPS * own, channels)
    results = [
        jax.ShapeDtypeStruct((own, height, across), BF),
        jax.ShapeDtypeStruct((TAPS, share, own), F32),
        jax.ShapeDtypeStruct((TAPS, share, own), F32),
    ]
    piece = cells // PIECES
    fold = lambda width: -(-width // 256) * 128
    scratch = [pltpu.VMEM((own, height, across), BF)] * 3
    scratch += [pltpu.VMEM((TAPS * own, channels), BF)] * 2
    scratch += [
        pltpu.VMEM((own * height, across), F32),
        pltpu.VMEM((PIECES, own, piece), F32),
        pltpu.VMEM((2, 3, PIECES, own, piece), BF),
        pltpu.VMEM((wide, cells + 2 * across), BF),
        pltpu.VMEM((2, 2, chips * own, wide), BF),
        pltpu.VMEM((2, groups, own, cells), BF),
        pltpu.VMEM((channels, cells), BF),
        pltpu.VMEM((2, 2, PIECES, chips * own, piece), F32),
        pltpu.VMEM((2, PIECES, chips * own, piece), F32),
        pltpu.VMEM((2, PIECES, chips, own, piece), BF),
        pltpu.VMEM((2, PIECES, chips - 1, own, piece), BF),
    ]
    for width in (cuts[0], cuts[1] - cuts[0]):
        scratch += [
            pltpu.VMEM((ZRUN, runs * share, width), F32),
            pltpu.VMEM((ZRUN, runs * share, width), BF),
            pltpu.VMEM((ZRUN - 1, runs * share, width), BF),
            pltpu.VMEM((runs, share, width), F32),
            pltpu.VMEM((runs - 1, share, width), F32),
        ]
    for width in (wide, wide - cuts[1]):
        scratch += [
            pltpu.VMEM((XRUN, halves, ZRUN * share, width), F32),
            pltpu.VMEM((XRUN, halves, ZRUN * share, width), BF),
            pltpu.VMEM((XRUN - 1, halves, ZRUN * share, width), BF),
            pltpu.VMEM((ZRUN, 2 * halves * share, fold(width)), F32),
            pltpu.VMEM((ZRUN, 2 * halves * share, fold(width)), BF),
            pltpu.VMEM((ZRUN - 1, 2 * halves * share, fold(width)), BF),
            pltpu.VMEM((halves, share, width), F32),
            pltpu.VMEM((halves - 1, share, width), F32),
        ]
    scratch.append(pltpu.SemaphoreType.DMA((5,)))
    for shape in (
        (2, PIECES, 2), (2, 2 * chips - 1), (2, PIECES), (2, PIECES, chips - 1), (2, ZRUN - 1), (2, runs - 1),
        (2, XRUN - 1), (2, ZRUN - 1), (2, halves - 1),
    ):
        scratch += [pltpu.SemaphoreType.DMA(shape), pltpu.SemaphoreType.DMA(shape)]
    arrays = (flat(inputs), flat(pre_acts), flat(out_grad), taps(weight_one), taps(weight_two))
    input_grad, one, two = pl.pallas_call(
        functools.partial(kernel, slabs, groups, own, height, cuts),
        out_shape=results,
        in_specs=[pl.BlockSpec(memory_space=pltpu.HBM)] * 5,
        out_specs=[pl.BlockSpec(memory_space=pltpu.VMEM)] * 3,
        scratch_shapes=scratch,
        compiler_params=pltpu.CompilerParams(
            collective_id=0, has_side_effects=True, vmem_limit_bytes=48 * 1024 * 1024
        ),
        name="conv_back",
    )(*[pltpu.with_memory_space_constraint(v, pltpu.HBM) for v in arrays])
    return input_grad.reshape(own, planes, height, across), one, two


def solution(mesh):
    in_specs = (
        P("af", "gz", None, None),
        P("af", "gz", None, None),
        P("af", "gz", None, None),
        P("af", None, None),
        P("af", None, None),
    )
    out_specs = (P("af", "gz", None, None), P(None, "gz", "af"), P(None, "gz", "af"))
    return jax.shard_map(
        functools.partial(body, mesh.shape["gz"], mesh.shape["af"]),
        mesh=mesh, in_specs=in_specs, out_specs=out_specs, check_vma=False,
    )
```

time: 72 us -> 66.2 us (0.919)
  the two profiles are of different devices: /device:TPU:8 before, /device:TPU:24 now
where the time goes in v2:
time: 66.2 us; the launch traced here: 66 us
  Pallas kernels  63.5 us (96%)
  local copies, waits for them, and re-layouts  1.88 us (3%)
    pallas_call x1, Pallas kernels, body(): pl.pallas_call(functools.partial(kernel, slabs, groups, own, height, cuts...  63.5 us
    unnamed x3, local copies, waits for them, and re-layouts  1.88 us

profile of v2, /device:TPU:24, one launch (start us, length us, event | category | flops | bytes accessed | tf_op | source)
XLA Modules:
  0.0 66.0 jit_solution(6483329183044053757)
XLA Ops:
  0.6 63.5 %conv_back.1 = (bf16[32,8,128]{2,1,0:T(8,128)(2,1)S(1)}, f32[27,4,32]{2,1,0:T(4,128)S(1)}, f32[27,4,32]{2,1,0:T(4,128)S(1)}) custom-call(bf16[32,8,128]{2,1,0:T(8,128)(2,1)} %bitcast.15, bf16[32,8,128]{2,1,0:T(8,128)(2,1)} %bitcast.16, bf16[32,8,128]{2,1,0:T(8,128)(2,1)} %bitcast.17, bf16[864,256]{1,0:T(8,128)(2,1)} %bitcast.13, bf16[864,256]{1,0:T(8,128)(2,1)} %bitcast.14), custom_call_target="tpu_custom_call" | custom-call | tf_op jit(solution)/shard_map/conv_back/pallas_call | solution.py:528
  64.2 0.6 copy.12
  64.8 0.6 copy.13
  65.4 0.6 copy.14

commit v3 on v2

--- a/solution.py
+++ b/solution.py
@@ -12,8 +12,8 @@
 F32 = jnp.float32
 ZRUN = 8
 XRUN = 4
-CUTS = (256, 512)
-PIECES = 4
+CUT = 256
+PIECES = 2
 ORDER = (0, -1, 1)
 TAPS = 27
 ACROSS = 128
@@ -21,13 +21,12 @@
 
 
 def kernel(
-    slabs, groups, own, height, cuts,
+    slabs, groups, own, height, cut,
     in_hbm, pre_hbm, og_hbm, w1_hbm, w2_hbm,
     ig_ref, f1_ref, f2_ref,
     in_ref, pre_ref, og_ref, w1_ref, w2_ref,
     rel, slope, field, G, WT, U, UP, PS, PR, SB, SR,
-    KF0, KS0, KR0, QS0, QR0,
-    KF1, KS1, KR1, QS1, QR1,
+    KF, KS, KR, QS, QR,
     XF0, XS0, XR0, ZF0, ZS0, ZR0, HS0, HR0,
     XF1, XS1, XR1, ZF1, ZS1, ZR1, HS1, HR1,
     load_s, halo_s, halo_r, ag_s, ag_r, px_s, px_r, y_s, y_r, k_s, k_r, q_s, q_r,
@@ -58,10 +57,8 @@
     part = cells // PIECES
     step = height // PIECES
     place = k % (ZRUN * XRUN)
-    edge = (place == 0) | (place == ZRUN * XRUN - 1)
     crossed = (place == ZRUN - 1) | (place == ZRUN * (XRUN - 1))
-    columns = ((0, wide), (cuts[-1], wide))
-    zbufs = ((KF0, KS0, KR0, QS0, QR0), (KF1, KS1, KR1, QS1, QR1))
+    columns = ((0, wide), (cut, wide))
     xbufs = ((XF0, XS0, XR0, ZF0, ZS0, ZR0, HS0, HR0), (XF1, XS1, XR1, ZF1, ZS1, ZR1, HS1, HR1))
 
     peers = [sibling, above, below]
@@ -190,8 +187,11 @@
                         G[tap_rows(number(a, b, c)), at_x(x + b + 1)] = s
 
     def grad_product(l, half, which, q):
-        at = slice(ACROSS + q * part, ACROSS + (q + 1) * part)
-        PS[l, half, q] = jnp.dot(WT[l, which], G[:, at], preferred_element_type=F32)
+        for n in range(0, part, 256):
+            at = slice(ACROSS + q * part + n, ACROSS + q * part + n + 256)
+            PS[l, half, q, :, n : n + 256] = jnp.dot(
+                WT[l, which], G[:, at], preferred_element_type=F32
+            )
 
     def grad_first(l, q):
         grad_product(l, 0, 1 - core, q)
@@ -229,14 +229,10 @@
             if block < TAPS:
                 out_ref[9 * (ORDER[block // 9] + 1) + block % 9] = total[:, i * own : (i + 1) * own]
 
-    zcolumns = ((0, cuts[0]), (cuts[0], cuts[1]))
-
-    def z_first(i):
-        KF, KS, KR = zbufs[i][:3]
-        start, stop = zcolumns[i]
-        for n in range(start, stop, 256):
-            size = min(256, stop - n)
-            at = slice(n - start, n - start + size)
+    def z_first():
+        for n in range(0, cut, 256):
+            size = min(256, cut - n)
+            at = slice(n, n + size)
             block = lax.dot_general(
                 UP[...], G[n : n + size, inner], last_dims, preferred_element_type=F32
             ).reshape(ZRUN, runs * share, size)
@@ -245,13 +241,12 @@
         return [
             send(
                 KS.at[lax.rem(z + d, ZRUN)], KR.at[d - 1],
-                k_s.at[i, d - 1], k_r.at[i, d - 1], z_at(d),
+                k_s.at[d - 1], k_r.at[d - 1], z_at(d),
             )
             for d in range(1, ZRUN)
         ]
 
-    def z_first_then(i, copies):
-        KF, KS, KR, QS, QR = zbufs[i]
+    def z_first_then(copies):
         for copy in copies:
             copy.wait_recv()
         for n in range(0, KF.shape[2], 128):
@@ -264,19 +259,18 @@
         return [
             send(
                 QS.at[lax.rem(run + d, runs)], QR.at[d - 1],
-                q_s.at[i, d - 1], q_r.at[i, d - 1], run_at(d),
+                q_s.at[d - 1], q_r.at[d - 1], run_at(d),
             )
             for d in range(1, runs)
         ]
 
-    def z_first_last(i, copies, out_ref):
-        QS, QR = zbufs[i][3:]
+    def z_first_last(copies, out_ref):
         for copy in copies:
             copy.wait_recv()
         total = QS[run]
         for d in range(runs - 1):
             total = total + QR[d]
-        by_tap(total, zcolumns[i][0], out_ref)
+        by_tap(total, 0, out_ref)
 
     def x_first(l):
         start, stop = columns[l]
@@ -387,7 +381,7 @@
         halo_send(0, q)
     gather_act, gather_in = gather_copies(0), gather_copies(1)
     gather_start(0, gather_act, jnp.logical_not(crossed))
-    gather_start(1, gather_in, edge)
+    gather_start(1, gather_in, jnp.logical_not(crossed))
 
     none = jnp.zeros((own, ACROSS), BF)
     for a in (-1, 0, 1):
@@ -419,44 +413,35 @@
     turn(0, w2_ref)
     parts = grad_pieces(0, lambda: None)
     gather_start(0, gather_act, crossed)
+    gather_start(1, gather_in, crossed)
     loads[4].wait()
     turn(1, w1_ref)
     onward = gather_forward(0, gather_act)
     gather_finish(onward)
     two = x_first(0)
+    onward = gather_forward(1, gather_in)
+    gather_finish(onward)
+    reorder(1)
     for q in range(PIECES):
         field[1, 1, q] = (grad_last(0, q, parts[q]) * slope[q]).astype(BF)
         halo_send(1, q)
-        if q == 0:
-            gather_start(1, gather_in, jnp.logical_not(edge))
     for q in range(PIECES):
         build(1, 1, q)
-    onward = gather_forward(1, gather_in)
-    gather_finish(onward)
-    reorder(1)
-    one_early = z_first(0)
+    one_z = z_first()
     two = x_first_then(0, two)
     late = []
-
-    def products():
-        late.append(x_first(1))
-        late.append(z_first(1))
-
-    parts = grad_pieces(1, products)
-    one_x, one_late = late
+    parts = grad_pieces(1, lambda: late.append(x_first(1)))
     two = x_first_pair(0, two)
-    one_early = z_first_then(0, one_early)
-    one_x = x_first_then(1, one_x)
-    one_late = z_first_then(1, one_late)
+    one_z = z_first_then(one_z)
+    one_x = x_first_then(1, late[0])
     x_first_last(0, two, f2_ref)
-    z_first_last(0, one_early, f1_ref)
+    z_first_last(one_z, f1_ref)
     for q in range(PIECES):
         total = grad_last(1, q, parts[q])
         for x in range(step):
             rel[pl.ds(q * step + x, own, stride=height), :] = total[:, at_x(x)]
     ig_ref[...] = rel[...].reshape(own, height, ACROSS).astype(BF)
     one_x = x_first_pair(1, one_x)
-    z_first_last(1, one_late, f1_ref)
     x_first_last(1, one_x, f1_ref)
     for l in range(2):
         for q in range(PIECES):
@@ -474,7 +459,7 @@
     halves = runs // XRUN
     share = channels // slabs
     wide = -(-TAPS * own // 128) * 128
-    cuts = CUTS
+    cut = CUT
     flat = lambda v: v.reshape(own, height, across)
     taps = lambda w: jnp.transpose(w, (1, 0, 2)).reshape(TAPS * own, channels)
     results = [
@@ -499,15 +484,14 @@
         pltpu.VMEM((2, PIECES, chips, own, piece), BF),
         pltpu.VMEM((2, PIECES, chips - 1, own, piece), BF),
     ]
-    for width in (cuts[0], cuts[1] - cuts[0]):
-        scratch += [
-            pltpu.VMEM((ZRUN, runs * share, width), F32),
-            pltpu.VMEM((ZRUN, runs * share, width), BF),
-            pltpu.VMEM((ZRUN - 1, runs * share, width), BF),
-            pltpu.VMEM((runs, share, width), F32),
-            pltpu.VMEM((runs - 1, share, width), F32),
-        ]
-    for width in (wide, wide - cuts[1]):
+    scratch += [
+        pltpu.VMEM((ZRUN, runs * share, cut), F32),
+        pltpu.VMEM((ZRUN, runs * share, cut), BF),
+        pltpu.VMEM((ZRUN - 1, runs * share, cut), BF),
+        pltpu.VMEM((runs, share, cut), F32),
+        pltpu.VMEM((runs - 1, share, cut), F32),
+    ]
+    for width in (wide, wide - cut):
         scratch += [
             pltpu.VMEM((XRUN, halves, ZRUN * share, width), F32),
             pltpu.VMEM((XRUN, halves, ZRUN * share, width), BF),
@@ -520,13 +504,13 @@
         ]
     scratch.append(pltpu.SemaphoreType.DMA((5,)))
     for shape in (
-        (2, PIECES, 2), (2, 2 * chips - 1), (2, PIECES), (2, PIECES, chips - 1), (2, ZRUN - 1), (2, runs - 1),
+        (2, PIECES, 2), (2, 2 * chips - 1), (2, PIECES), (2, PIECES, chips - 1), (ZRUN - 1,), (runs - 1,),
         (2, XRUN - 1), (2, ZRUN - 1), (2, halves - 1),
     ):
         scratch += [pltpu.SemaphoreType.DMA(shape), pltpu.SemaphoreType.DMA(shape)]
     arrays = (flat(inputs), flat(pre_acts), flat(out_grad), taps(weight_one), taps(weight_two))
     input_grad, one, two = pl.pallas_call(
-        functools.partial(kernel, slabs, groups, own, height, cuts),
+        functools.partial(kernel, slabs, groups, own, height, cut),
         out_shape=results,
         in_specs=[pl.BlockSpec(memory_space=pltpu.HBM)] * 5,
         out_specs=[pl.BlockSpec(memory_space=pltpu.VMEM)] * 3,

time: 66.2 us -> 67.1 us (1.014)
  Pallas kernels: 63.5 us -> 64.5 us
    pallas_call x1, Pallas kernels: 63.5 us -> 64.5 us  [body(): pl.pallas_call(functools.partial(kernel, slabs, groups, own, height, cut)...]
where the time goes in v3:
time: 67.1 us; the launch traced here: 67 us
  Pallas kernels  64.5 us (96%)
  local copies, waits for them, and re-layouts  1.88 us (3%)
    pallas_call x1, Pallas kernels, body(): pl.pallas_call(functools.partial(kernel, slabs, groups, own, height, cut)...  64.5 us
    unnamed x3, local copies, waits for them, and re-layouts  1.88 us

profile of v3, /device:TPU:24, one launch (start us, length us, event | category | flops | bytes accessed | tf_op | source)
XLA Modules:
  0.0 67.0 jit_solution(9920348870511980224)
XLA Ops:
  0.6 64.5 %conv_back.1 = (bf16[32,8,128]{2,1,0:T(8,128)(2,1)S(1)}, f32[27,4,32]{2,1,0:T(4,128)S(1)}, f32[27,4,32]{2,1,0:T(4,128)S(1)}) custom-call(bf16[32,8,128]{2,1,0:T(8,128)(2,1)} %bitcast.15, bf16[32,8,128]{2,1,0:T(8,128)(2,1)} %bitcast.16, bf16[32,8,128]{2,1,0:T(8,128)(2,1)} %bitcast.17, bf16[864,256]{1,0:T(8,128)(2,1)} %bitcast.13, bf16[864,256]{1,0:T(8,128)(2,1)} %bitcast.14), custom_call_target="tpu_custom_call" | custom-call | tf_op jit(solution)/shard_map/conv_back/pallas_call | solution.py:512
  65.1 0.6 copy.12
  65.7 0.6 copy.13
  66.3 0.6 copy.14

commit v4 on v3

--- a/solution.py
+++ b/solution.py
@@ -12,7 +12,7 @@
 F32 = jnp.float32
 ZRUN = 8
 XRUN = 4
-CUT = 256
+CUT = 384
 PIECES = 2
 ORDER = (0, -1, 1)
 TAPS = 27
@@ -56,6 +56,19 @@
     inner = slice(ACROSS, ACROSS + cells)
     part = cells // PIECES
     step = height // PIECES
+    sibling = {"af": chip * 2 + (1 - core)}
+    chip_at = lambda d: {"af": lax.rem(chip + d, chips) * 2 + core}
+    z_at = lambda d: {"gz": run * ZRUN + lax.rem(z + d, ZRUN)}
+    run_at = lambda d: {"gz": lax.rem(run + d, runs) * ZRUN + z}
+    x_at = lambda d: {"gz": (hi * XRUN + lax.rem(xi + d, XRUN)) * ZRUN + z}
+    hi_at = lambda d: {"gz": (lax.rem(hi + d, halves) * XRUN + xi) * ZRUN + z}
+    above = {"gz": lax.rem(k + 1, slabs)}
+    below = {"gz": lax.rem(k + slabs - 1, slabs)}
+    filled = TAPS * own
+    wide = G.shape[0]
+    inner = slice(ACROSS, ACROSS + cells)
+    part = cells // PIECES
+    step = height // PIECES
     place = k % (ZRUN * XRUN)
     crossed = (place == ZRUN - 1) | (place == ZRUN * (XRUN - 1))
     columns = ((0, wide), (cut, wide))
@@ -117,25 +130,22 @@
         pl.when(k < slabs - 1)(up.wait_send)
         pl.when(k > 0)(down.wait_send)
 
-    def gather_copies(l):
+    def gather_start(l, low, high):
+        mine = U.at[l, me, pl.ds(low, high - low)]
+        i = l if low == 0 else 2
+        return [
+            send(mine, mine, ag_s.at[i, d], ag_r.at[i, d], chip_at(d)) for d in range(1, chips)
+        ]
+
+    def gather_sibling(l):
         mine = U.at[l, me]
-        found = [
-            remote(mine, mine, ag_s.at[l, d], ag_r.at[l, d], chip_at(d)) for d in range(1, chips)
-        ]
-        found.append(remote(mine, mine, ag_s.at[l, 0], ag_r.at[l, 0], sibling))
-        return found
-
-    def gather_start(l, found, when):
-        @pl.when(when)
-        def _():
-            for copy in found:
-                copy.start()
-
-    def gather_forward(l, found):
-        started.extend(found)
-        onward = [found[-1]]
+        return send(mine, mine, ag_s.at[l, 0], ag_r.at[l, 0], sibling)
+
+    def gather_forward(l, *found):
+        onward = []
         for d in range(1, chips):
-            found[d - 1].wait_recv()
+            for copies in found:
+                copies[d - 1].wait_recv()
             block = U.at[l, lax.rem(chip + chips - d, chips) * 2 + core]
             onward.append(
                 send(block, block, ag_s.at[l, chips - 1 + d], ag_r.at[l, chips - 1 + d], sibling)
@@ -193,11 +203,14 @@
                 WT[l, which], G[:, at], preferred_element_type=F32
             )
 
-    def grad_first(l, q):
-        grad_product(l, 0, 1 - core, q)
-        copy = send(PS.at[l, 0, q], PR.at[l, q], px_s.at[l, q], px_r.at[l, q], sibling)
-        grad_product(l, 1, core, q)
-        return copy
+    def grad_first(l):
+        copies = []
+        for q in range(PIECES):
+            grad_product(l, 0, 1 - core, q)
+            copies.append(send(PS.at[l, 0, q], PR.at[l, q], px_s.at[l, q], px_r.at[l, q], sibling))
+        for q in range(PIECES):
+            grad_product(l, 1, core, q)
+        return copies
 
     def grad_second(l, q, copy):
         copy.wait_recv()
@@ -379,9 +392,9 @@
     pl.semaphore_wait(barrier, len(peers))
     for q in range(PIECES):
         halo_send(0, q)
-    gather_act, gather_in = gather_copies(0), gather_copies(1)
-    gather_start(0, gather_act, jnp.logical_not(crossed))
-    gather_start(1, gather_in, jnp.logical_not(crossed))
+    gather_act = gather_start(0, 0, own)
+    near_act = gather_sibling(0)
+    gather_in = gather_start(1, 0, own // 2)
 
     none = jnp.zeros((own, ACROSS), BF)
     for a in (-1, 0, 1):
@@ -391,57 +404,51 @@
     if wide > filled:
         G[filled:, :] = jnp.zeros((wide - filled, G.shape[1]), BF)
 
-    def grad_pieces(l, last):
-        pair, parts = [], []
+    def finish_taps(l):
         for q in range(PIECES):
             halo_wait(l, q)
             build(l, 0, q)
             build(l, 2, q)
-            if q > 0:
-                pair.append(grad_first(l, q - 1))
-            if q > 1:
-                parts.append(grad_second(l, q - 2, pair[q - 2]))
-        pair.append(grad_first(l, PIECES - 1))
-        last()
-        for q in range(PIECES - 2, PIECES):
-            parts.append(grad_second(l, q, pair[q]))
-        return parts
 
     for q in range(PIECES):
         build(0, 1, q)
     loads[2].wait()
     turn(0, w2_ref)
-    parts = grad_pieces(0, lambda: None)
-    gather_start(0, gather_act, crossed)
-    gather_start(1, gather_in, crossed)
+    finish_taps(0)
+    pair = grad_first(0)
+    parts = [grad_second(0, q, pair[q]) for q in range(PIECES)]
+    onward = gather_forward(0, gather_act)
     loads[4].wait()
     turn(1, w1_ref)
-    onward = gather_forward(0, gather_act)
-    gather_finish(onward)
+    gather_finish(onward + [near_act])
     two = x_first(0)
-    onward = gather_forward(1, gather_in)
-    gather_finish(onward)
-    reorder(1)
     for q in range(PIECES):
         field[1, 1, q] = (grad_last(0, q, parts[q]) * slope[q]).astype(BF)
         halo_send(1, q)
+    gather_rest = gather_start(1, own // 2, own)
+    near_in = gather_sibling(1)
     for q in range(PIECES):
         build(1, 1, q)
+    finish_taps(1)
+    pair = grad_first(1)
+    onward = gather_forward(1, gather_in, gather_rest)
+    gather_finish(onward + [near_in])
+    one_x = x_first(1)
+    reorder(1)
     one_z = z_first()
+    parts = [grad_second(1, q, pair[q]) for q in range(PIECES)]
     two = x_first_then(0, two)
-    late = []
-    parts = grad_pieces(1, lambda: late.append(x_first(1)))
+    one_x = x_first_then(1, one_x)
+    one_z = z_first_then(one_z)
     two = x_first_pair(0, two)
-    one_z = z_first_then(one_z)
-    one_x = x_first_then(1, late[0])
-    x_first_last(0, two, f2_ref)
-    z_first_last(one_z, f1_ref)
     for q in range(PIECES):
         total = grad_last(1, q, parts[q])
         for x in range(step):
             rel[pl.ds(q * step + x, own, stride=height), :] = total[:, at_x(x)]
     ig_ref[...] = rel[...].reshape(own, height, ACROSS).astype(BF)
     one_x = x_first_pair(1, one_x)
+    x_first_last(0, two, f2_ref)
+    z_first_last(one_z, f1_ref)
     x_first_last(1, one_x, f1_ref)
     for l in range(2):
         for q in range(PIECES):
@@ -504,7 +511,7 @@
         ]
     scratch.append(pltpu.SemaphoreType.DMA((5,)))
     for shape in (
-        (2, PIECES, 2), (2, 2 * chips - 1), (2, PIECES), (2, PIECES, chips - 1), (ZRUN - 1,), (runs - 1,),
+        (2, PIECES, 2), (3, 2 * chips - 1), (2, PIECES), (2, PIECES, chips - 1), (ZRUN - 1,), (runs - 1,),
         (2, XRUN - 1), (2, ZRUN - 1), (2, halves - 1),
     ):
         scratch += [pltpu.SemaphoreType.DMA(shape), pltpu.SemaphoreType.DMA(shape)]

time: 67.1 us -> 62.5 us (0.931)
  Pallas kernels: 64.5 us -> 59.8 us
    pallas_call x1, Pallas kernels: 64.5 us -> 59.8 us  [body(): pl.pallas_call(functools.partial(kernel, slabs, groups, own, height, cut)...]
where the time goes in v4:
time: 62.5 us; the launch traced here: 62.4 us
  Pallas kernels  59.8 us (96%)
  local copies, waits for them, and re-layouts  1.88 us (3%)
  between operations  0.64 us (1%)
    pallas_call x1, Pallas kernels, body(): pl.pallas_call(functools.partial(kernel, slabs, groups, own, height, cut)...  59.8 us
    unnamed x3, local copies, waits for them, and re-layouts  1.88 us

profile of v4, /device:TPU:24, one launch (start us, length us, event | category | flops | bytes accessed | tf_op | source)
XLA Modules:
  0.0 62.4 jit_solution(17132506774689162254)
XLA Ops:
  0.6 59.8 %conv_back.1 = (bf16[32,8,128]{2,1,0:T(8,128)(2,1)S(1)}, f32[27,4,32]{2,1,0:T(4,128)S(1)}, f32[27,4,32]{2,1,0:T(4,128)S(1)}) custom-call(bf16[32,8,128]{2,1,0:T(8,128)(2,1)} %bitcast.15, bf16[32,8,128]{2,1,0:T(8,128)(2,1)} %bitcast.16, bf16[32,8,128]{2,1,0:T(8,128)(2,1)} %bitcast.17, bf16[864,256]{1,0:T(8,128)(2,1)} %bitcast.13, bf16[864,256]{1,0:T(8,128)(2,1)} %bitcast.14), custom_call_target="tpu_custom_call" | custom-call | tf_op jit(solution)/shard_map/conv_back/pallas_call | solution.py:519
  60.5 0.6 %copy.12 = bf16[32,1,8,128]{3,2,1,0:T(8,128)(2,1)} copy(bf16[32,1,8,128]{3,2,1,0:T(8,128)(2,1)S(1)} %bitcast.12) | data formatting | bytes 131072
  61.1 0.6 copy.13
  61.7 0.6 copy.14

commit v5 on v4

--- a/solution.py
+++ b/solution.py
@@ -43,6 +43,10 @@
     chip, core = me // 2, me % 2
     run, z = k // ZRUN, k % ZRUN
     hi, xi = run // XRUN, run % XRUN
+    place = k % (ZRUN * XRUN)
+    ends = (k == 0) | (k == slabs - 1)
+    border = ((place == 0) | (place == ZRUN * XRUN - 1)) & jnp.logical_not(ends)
+    inland = jnp.logical_not(ends | border)
     sibling = {"af": chip * 2 + (1 - core)}
     chip_at = lambda d: {"af": lax.rem(chip + d, chips) * 2 + core}
     z_at = lambda d: {"gz": run * ZRUN + lax.rem(z + d, ZRUN)}
@@ -56,23 +60,15 @@
     inner = slice(ACROSS, ACROSS + cells)
     part = cells // PIECES
     step = height // PIECES
-    sibling = {"af": chip * 2 + (1 - core)}
-    chip_at = lambda d: {"af": lax.rem(chip + d, chips) * 2 + core}
-    z_at = lambda d: {"gz": run * ZRUN + lax.rem(z + d, ZRUN)}
-    run_at = lambda d: {"gz": lax.rem(run + d, runs) * ZRUN + z}
-    x_at = lambda d: {"gz": (hi * XRUN + lax.rem(xi + d, XRUN)) * ZRUN + z}
-    hi_at = lambda d: {"gz": (lax.rem(hi + d, halves) * XRUN + xi) * ZRUN + z}
-    above = {"gz": lax.rem(k + 1, slabs)}
-    below = {"gz": lax.rem(k + slabs - 1, slabs)}
-    filled = TAPS * own
-    wide = G.shape[0]
-    inner = slice(ACROSS, ACROSS + cells)
-    part = cells // PIECES
-    step = height // PIECES
-    place = k % (ZRUN * XRUN)
-    crossed = (place == ZRUN - 1) | (place == ZRUN * (XRUN - 1))
     columns = ((0, wide), (cut, wide))
     xbufs = ((XF0, XS0, XR0, ZF0, ZS0, ZR0, HS0, HR0), (XF1, XS1, XR1, ZF1, ZS1, ZR1, HS1, HR1))
+
+    loads = []
+    for i, (src, dst) in enumerate(
+        ((og_hbm, og_ref), (pre_hbm, pre_ref), (w2_hbm, w2_ref), (in_hbm, in_ref), (w1_hbm, w1_ref))
+    ):
+        loads.append(pltpu.make_async_copy(src, dst, load_s.at[i]))
+        loads[-1].start()
 
     peers = [sibling, above, below]
     peers += [chip_at(d) for d in range(1, chips)]
@@ -82,13 +78,6 @@
     for peer in peers:
         pl.semaphore_signal(barrier, inc=1, device_id=peer, device_id_type=MESH)
 
-    loads = []
-    for i, (src, dst) in enumerate(
-        ((og_hbm, og_ref), (pre_hbm, pre_ref), (w2_hbm, w2_ref), (in_hbm, in_ref), (w1_hbm, w1_ref))
-    ):
-        loads.append(pltpu.make_async_copy(src, dst, load_s.at[i]))
-        loads[-1].start()
-
     started = []
 
     def remote(src, dst, s, r, to):
@@ -130,12 +119,20 @@
         pl.when(k < slabs - 1)(up.wait_send)
         pl.when(k > 0)(down.wait_send)
 
-    def gather_start(l, low, high):
+    def gather_copies(l, low, high):
         mine = U.at[l, me, pl.ds(low, high - low)]
         i = l if low == 0 else 2
-        return [
-            send(mine, mine, ag_s.at[i, d], ag_r.at[i, d], chip_at(d)) for d in range(1, chips)
-        ]
+        found = [
+            remote(mine, mine, ag_s.at[i, d], ag_r.at[i, d], chip_at(d)) for d in range(1, chips)
+        ]
+        started.extend(found)
+        return found
+
+    def start_when(when, copies):
+        @pl.when(when)
+        def _():
+            for copy in copies:
+                copy.start()
 
     def gather_sibling(l):
         mine = U.at[l, me]
@@ -208,9 +205,11 @@
         for q in range(PIECES):
             grad_product(l, 0, 1 - core, q)
             copies.append(send(PS.at[l, 0, q], PR.at[l, q], px_s.at[l, q], px_r.at[l, q], sibling))
+        return copies
+
+    def grad_own(l):
         for q in range(PIECES):
             grad_product(l, 1, core, q)
-        return copies
 
     def grad_second(l, q, copy):
         copy.wait_recv()
@@ -371,30 +370,32 @@
     loads[0].wait()
     for x, v in enumerate(planes_of(og_ref)):
         field[0, 1, x // step, :, at_x(x % step)] = v.astype(BF)
+
+    @pl.when(k == 0)
+    def _():
+        for l in range(2):
+            field[l, 0] = jnp.zeros(field.shape[2:], BF)
+
+    @pl.when(k == slabs - 1)
+    def _():
+        for l in range(2):
+            field[l, 2] = jnp.zeros(field.shape[2:], BF)
+
+    pl.semaphore_wait(barrier, len(peers))
+    for q in range(PIECES):
+        halo_send(0, q)
     loads[1].wait()
     for x, v in enumerate(planes_of(pre_ref)):
         slope[x // step, :, at_x(x % step)] = jnp.where(v > 0, jnp.float32(1.0), jnp.float32(0.3))
         U[0, me, :, at_x(x)] = jnp.where(v > 0, v, 0.3 * v).astype(BF)
+    gather_act = gather_copies(0, 0, own)
+    start_when(jnp.logical_not(ends), gather_act)
+    near_act = gather_sibling(0)
     loads[3].wait()
     for x, v in enumerate(planes_of(in_ref)):
         U[1, me, :, at_x(x)] = v.astype(BF)
-
-    @pl.when(k == 0)
-    def _():
-        for l in range(2):
-            field[l, 0] = jnp.zeros(field.shape[2:], BF)
-
-    @pl.when(k == slabs - 1)
-    def _():
-        for l in range(2):
-            field[l, 2] = jnp.zeros(field.shape[2:], BF)
-
-    pl.semaphore_wait(barrier, len(peers))
-    for q in range(PIECES):
-        halo_send(0, q)
-    gather_act = gather_start(0, 0, own)
-    near_act = gather_sibling(0)
-    gather_in = gather_start(1, 0, own // 2)
+    gather_in = gather_copies(1, 0, own // 2)
+    start_when(inland, gather_in)
 
     none = jnp.zeros((own, ACROSS), BF)
     for a in (-1, 0, 1):
@@ -415,8 +416,11 @@
     loads[2].wait()
     turn(0, w2_ref)
     finish_taps(0)
+    start_when(border, gather_in)
     pair = grad_first(0)
+    grad_own(0)
     parts = [grad_second(0, q, pair[q]) for q in range(PIECES)]
+    start_when(ends, gather_act + gather_in)
     onward = gather_forward(0, gather_act)
     loads[4].wait()
     turn(1, w1_ref)
@@ -425,17 +429,20 @@
     for q in range(PIECES):
         field[1, 1, q] = (grad_last(0, q, parts[q]) * slope[q]).astype(BF)
         halo_send(1, q)
-    gather_rest = gather_start(1, own // 2, own)
+    gather_rest = gather_copies(1, own // 2, own)
+    for copy in gather_rest:
+        copy.start()
     near_in = gather_sibling(1)
     for q in range(PIECES):
         build(1, 1, q)
+    onward = gather_forward(1, gather_in, gather_rest)
     finish_taps(1)
     pair = grad_first(1)
-    onward = gather_forward(1, gather_in, gather_rest)
     gather_finish(onward + [near_in])
     one_x = x_first(1)
     reorder(1)
     one_z = z_first()
+    grad_own(1)
     parts = [grad_second(1, q, pair[q]) for q in range(PIECES)]
     two = x_first_then(0, two)
     one_x = x_first_then(1, one_x)
@@ -449,12 +456,12 @@
     one_x = x_first_pair(1, one_x)
     x_first_last(0, two, f2_ref)
     z_first_last(one_z, f1_ref)
-    x_first_last(1, one_x, f1_ref)
     for l in range(2):
         for q in range(PIECES):
             halo_done(l, q)
     for copy in started:
         copy.wait_send()
+    x_first_last(1, one_x, f1_ref)
 
 
 def body(slabs, groups, inputs, pre_acts, out_grad, weight_one, weight_two):

time: 62.5 us -> 62.4 us (level)
  no operation moved by 1% of the time
where the time goes in v5:
time: 62.4 us; the launch traced here: 62.3 us
  Pallas kernels  59.8 us (96%)
  local copies, waits for them, and re-layouts  1.88 us (3%)
  between operations  0.64 us (1%)
    pallas_call x1, Pallas kernels, body(): pl.pallas_call(functools.partial(kernel, slabs, groups, own, height, cut)...  59.8 us
    unnamed x3, local copies, waits for them, and re-layouts  1.88 us

profile of v5, /device:TPU:24, one launch (start us, length us, event | category | flops | bytes accessed | tf_op | source)
XLA Modules:
  0.0 62.3 jit_solution(15465578755286249037)
XLA Ops:
  0.6 59.8 %conv_back.1 = (bf16[32,8,128]{2,1,0:T(8,128)(2,1)S(1)}, f32[27,4,32]{2,1,0:T(4,128)S(1)}, f32[27,4,32]{2,1,0:T(4,128)S(1)}) custom-call(bf16[32,8,128]{2,1,0:T(8,128)(2,1)} %bitcast.15, bf16[32,8,128]{2,1,0:T(8,128)(2,1)} %bitcast.16, bf16[32,8,128]{2,1,0:T(8,128)(2,1)} %bitcast.17, bf16[864,256]{1,0:T(8,128)(2,1)} %bitcast.13, bf16[864,256]{1,0:T(8,128)(2,1)} %bitcast.14), custom_call_target="tpu_custom_call" | custom-call | tf_op jit(solution)/shard_map/conv_back/pallas_call | solution.py:526
  60.4 0.6 %copy.12 = bf16[32,1,8,128]{3,2,1,0:T(8,128)(2,1)} copy(bf16[32,1,8,128]{3,2,1,0:T(8,128)(2,1)S(1)} %bitcast.12) | data formatting | bytes 131072
  61.0 0.6 copy.13
  61.7 0.6 copy.14

commit v6 on v5

--- a/solution.py
+++ b/solution.py
@@ -25,7 +25,7 @@
     in_hbm, pre_hbm, og_hbm, w1_hbm, w2_hbm,
     ig_ref, f1_ref, f2_ref,
     in_ref, pre_ref, og_ref, w1_ref, w2_ref,
-    rel, slope, field, G, WT, U, UP, PS, PR, SB, SR,
+    rel, slope, field, G, WT, U, UP, PB, PS, PR, SB, SR,
     KF, KS, KR, QS, QR,
     XF0, XS0, XR0, ZF0, ZS0, ZR0, HS0, HR0,
     XF1, XS1, XR1, ZF1, ZS1, ZR1, HS1, HR1,
@@ -193,30 +193,29 @@
                     if 0 <= x + b < height:
                         G[tap_rows(number(a, b, c)), at_x(x + b + 1)] = s
 
-    def grad_product(l, half, which, q):
+    def grad_product(l, which, q, to):
         for n in range(0, part, 256):
             at = slice(ACROSS + q * part + n, ACROSS + q * part + n + 256)
-            PS[l, half, q, :, n : n + 256] = jnp.dot(
-                WT[l, which], G[:, at], preferred_element_type=F32
-            )
+            block = jnp.dot(WT[l, which], G[:, at], preferred_element_type=F32)
+            to[l, q, :, n : n + 256] = block.astype(to.dtype)
 
     def grad_first(l):
         copies = []
         for q in range(PIECES):
-            grad_product(l, 0, 1 - core, q)
-            copies.append(send(PS.at[l, 0, q], PR.at[l, q], px_s.at[l, q], px_r.at[l, q], sibling))
+            grad_product(l, 1 - core, q, PB)
+            copies.append(send(PB.at[l, q], PR.at[l, q], px_s.at[l, q], px_r.at[l, q], sibling))
         return copies
 
     def grad_own(l):
         for q in range(PIECES):
-            grad_product(l, 1, core, q)
+            grad_product(l, core, q, PS)
 
     def grad_second(l, q, copy):
         copy.wait_recv()
         for j in range(chips):
             at = slice(j * own, (j + 1) * own)
-            total = PS[l, 1, q, at, :] + PR[l, q, at, :]
-            PS[l, 1, q, at, :] = total
+            total = PS[l, q, at, :] + PR[l, q, at, :].astype(F32)
+            PS[l, q, at, :] = total
             SB[l, q, j] = total.astype(BF)
         return [
             send(
@@ -230,7 +229,7 @@
         for copy in found:
             copy.wait_recv()
         mine = pl.ds(pl.multiple_of(chip * own, own), own)
-        total = PS[l, 1, q, mine, :]
+        total = PS[l, q, mine, :]
         for d in range(chips - 1):
             total = total + SR[l, q, d].astype(F32)
         return total
@@ -438,13 +437,13 @@
     onward = gather_forward(1, gather_in, gather_rest)
     finish_taps(1)
     pair = grad_first(1)
+    two = x_first_then(0, two)
     gather_finish(onward + [near_in])
     one_x = x_first(1)
     reorder(1)
     one_z = z_first()
     grad_own(1)
     parts = [grad_second(1, q, pair[q]) for q in range(PIECES)]
-    two = x_first_then(0, two)
     one_x = x_first_then(1, one_x)
     one_z = z_first_then(one_z)
     two = x_first_pair(0, two)
@@ -493,8 +492,9 @@
         pltpu.VMEM((2, 2, chips * own, wide), BF),
         pltpu.VMEM((2, groups, own, cells), BF),
         pltpu.VMEM((channels, cells), BF),
-        pltpu.VMEM((2, 2, PIECES, chips * own, piece), F32),
+        pltpu.VMEM((2, PIECES, chips * own, piece), BF),
         pltpu.VMEM((2, PIECES, chips * own, piece), F32),
+        pltpu.VMEM((2, PIECES, chips * own, piece), BF),
         pltpu.VMEM((2, PIECES, chips, own, piece), BF),
         pltpu.VMEM((2, PIECES, chips - 1, own, piece), BF),
     ]

time: 62.4 us -> 62.1 us (level)
  no operation moved by 1% of the time
where the time goes in v6:
time: 62.1 us; the launch traced here: 62 us
  Pallas kernels  59.5 us (96%)
  local copies, waits for them, and re-layouts  1.88 us (3%)
  between operations  0.64 us (1%)
    pallas_call x1, Pallas kernels, body(): pl.pallas_call(functools.partial(kernel, slabs, groups, own, height, cut)...  59.5 us
    unnamed x3, local copies, waits for them, and re-layouts  1.88 us

profile of v6, /device:TPU:24, one launch (start us, length us, event | category | flops | bytes accessed | tf_op | source)
XLA Modules:
  0.0 62.0 jit_solution(8029477252850862009)
XLA Ops:
  0.6 59.5 %conv_back.1 = (bf16[32,8,128]{2,1,0:T(8,128)(2,1)S(1)}, f32[27,4,32]{2,1,0:T(4,128)S(1)}, f32[27,4,32]{2,1,0:T(4,128)S(1)}) custom-call(bf16[32,8,128]{2,1,0:T(8,128)(2,1)} %bitcast.15, bf16[32,8,128]{2,1,0:T(8,128)(2,1)} %bitcast.16, bf16[32,8,128]{2,1,0:T(8,128)(2,1)} %bitcast.17, bf16[864,256]{1,0:T(8,128)(2,1)} %bitcast.13, bf16[864,256]{1,0:T(8,128)(2,1)} %bitcast.14), custom_call_target="tpu_custom_call" | custom-call | tf_op jit(solution)/shard_map/conv_back/pallas_call | solution.py:526
  60.1 0.6 %copy.12 = bf16[32,1,8,128]{3,2,1,0:T(8,128)(2,1)} copy(bf16[32,1,8,128]{3,2,1,0:T(8,128)(2,1)S(1)} %bitcast.12) | data formatting | bytes 131072
  60.8 0.6 %copy.13 = f32[27,4,32]{2,1,0:T(4,128)} copy(f32[27,4,32]{2,1,0:T(4,128)S(1)} %get-tuple-element.16) | data formatting | bytes 27648
  61.4 0.6 %copy.14 = f32[27,4,32]{2,1,0:T(4,128)} copy(f32[27,4,32]{2,1,0:T(4,128)S(1)} %get-tuple-element.17) | data formatting | bytes 27648

commit v7 on v6

--- a/solution.py
+++ b/solution.py
@@ -50,7 +50,6 @@
     sibling = {"af": chip * 2 + (1 - core)}
     chip_at = lambda d: {"af": lax.rem(chip + d, chips) * 2 + core}
     z_at = lambda d: {"gz": run * ZRUN + lax.rem(z + d, ZRUN)}
-    run_at = lambda d: {"gz": lax.rem(run + d, runs) * ZRUN + z}
     x_at = lambda d: {"gz": (hi * XRUN + lax.rem(xi + d, XRUN)) * ZRUN + z}
     hi_at = lambda d: {"gz": (lax.rem(hi + d, halves) * XRUN + xi) * ZRUN + z}
     above = {"gz": lax.rem(k + 1, slabs)}
@@ -73,7 +72,8 @@
     peers = [sibling, above, below]
     peers += [chip_at(d) for d in range(1, chips)]
     peers += [z_at(d) for d in range(1, ZRUN)]
-    peers += [run_at(d) for d in range(1, runs)]
+    peers += [x_at(d) for d in range(1, XRUN)]
+    peers += [hi_at(d) for d in range(1, halves)]
     barrier = pltpu.get_barrier_semaphore()
     for peer in peers:
         pl.semaphore_signal(barrier, inc=1, device_id=peer, device_id_type=MESH)
@@ -196,8 +196,9 @@
     def grad_product(l, which, q, to):
         for n in range(0, part, 256):
             at = slice(ACROSS + q * part + n, ACROSS + q * part + n + 256)
-            block = jnp.dot(WT[l, which], G[:, at], preferred_element_type=F32)
-            to[l, q, :, n : n + 256] = block.astype(to.dtype)
+            to[l, q, :, n : n + 256] = jnp.dot(
+                WT[l, which], G[:, at], preferred_element_type=F32
+            )
 
     def grad_first(l):
         copies = []
@@ -214,7 +215,7 @@
         copy.wait_recv()
         for j in range(chips):
             at = slice(j * own, (j + 1) * own)
-            total = PS[l, q, at, :] + PR[l, q, at, :].astype(F32)
+            total = PS[l, q, at, :] + PR[l, q, at, :]
             PS[l, q, at, :] = total
             SB[l, q, j] = total.astype(BF)
         return [
@@ -234,11 +235,10 @@
             total = total + SR[l, q, d].astype(F32)
         return total
 
-    def by_tap(total, start, out_ref):
-        for i in range(total.shape[1] // own):
-            block = start // own + i
-            if block < TAPS:
-                out_ref[9 * (ORDER[block // 9] + 1) + block % 9] = total[:, i * own : (i + 1) * own]
+    def by_tap(total, out_ref):
+        for block in range(TAPS):
+            at = slice(block * own, (block + 1) * own)
+            out_ref[9 * (ORDER[block // 9] + 1) + block % 9] = total[:, at]
 
     def z_first():
         for n in range(0, cut, 256):
@@ -266,22 +266,25 @@
             for d in range(ZRUN - 1):
                 total = total + KR[d, :, at].astype(F32)
             for j in range(runs):
-                QS[j, :, at] = total[j * share : (j + 1) * share, :]
+                h, x = divmod(j, XRUN)
+                part_rows = total[j * share : (j + 1) * share, :]
+                QS[x, h * share : (h + 1) * share, at] = part_rows
         return [
             send(
-                QS.at[lax.rem(run + d, runs)], QR.at[d - 1],
-                q_s.at[d - 1], q_r.at[d - 1], run_at(d),
-            )
-            for d in range(1, runs)
-        ]
-
-    def z_first_last(copies, out_ref):
+                QS.at[lax.rem(xi + d, XRUN)], QR.at[d - 1],
+                q_s.at[d - 1], q_r.at[d - 1], x_at(d),
+            )
+            for d in range(1, XRUN)
+        ]
+
+    def z_first_pair(copies):
         for copy in copies:
             copy.wait_recv()
-        total = QS[run]
-        for d in range(runs - 1):
+        total = QS[xi]
+        for d in range(XRUN - 1):
             total = total + QR[d]
-        by_tap(total, 0, out_ref)
+        for h in range(halves):
+            HS1[h, :, :cut] = total[h * share : (h + 1) * share, :]
 
     def x_first(l):
         start, stop = columns[l]
@@ -345,9 +348,12 @@
             total = total + ZR[d].astype(F32)
         fold = total.shape[1]
         for h in range(halves):
-            HS[h, :, :fold] = total[h * share : (h + 1) * share, :]
+            HS[h, :, start : start + fold] = total[h * share : (h + 1) * share, :]
             rest = stop - start - fold
-            HS[h, :, fold:] = total[eight + h * share : eight + (h + 1) * share, :rest]
+            HS[h, :, start + fold :] = total[eight + h * share : eight + (h + 1) * share, :rest]
+
+    def last_start(l):
+        HS, HR = xbufs[l][6:]
         return [
             send(
                 HS.at[lax.rem(hi + d, halves)], HR.at[d - 1],
@@ -356,15 +362,14 @@
             for d in range(1, halves)
         ]
 
-    def x_first_last(l, copies, out_ref):
-        start, stop = columns[l]
+    def last_finish(l, copies, out_ref):
         HS, HR = xbufs[l][6:]
         for copy in copies:
             copy.wait_recv()
         total = HS[hi]
         for d in range(halves - 1):
             total = total + HR[d]
-        by_tap(total, start, out_ref)
+        by_tap(total, out_ref)
 
     loads[0].wait()
     for x, v in enumerate(planes_of(og_ref)):
@@ -439,28 +444,30 @@
     pair = grad_first(1)
     two = x_first_then(0, two)
     gather_finish(onward + [near_in])
-    one_x = x_first(1)
     reorder(1)
     one_z = z_first()
+    one_x = x_first(1)
     grad_own(1)
     parts = [grad_second(1, q, pair[q]) for q in range(PIECES)]
+    x_first_pair(0, two)
+    two = last_start(0)
     one_x = x_first_then(1, one_x)
     one_z = z_first_then(one_z)
-    two = x_first_pair(0, two)
     for q in range(PIECES):
         total = grad_last(1, q, parts[q])
         for x in range(step):
             rel[pl.ds(q * step + x, own, stride=height), :] = total[:, at_x(x)]
     ig_ref[...] = rel[...].reshape(own, height, ACROSS).astype(BF)
-    one_x = x_first_pair(1, one_x)
-    x_first_last(0, two, f2_ref)
-    z_first_last(one_z, f1_ref)
+    last_finish(0, two, f2_ref)
+    z_first_pair(one_z)
+    x_first_pair(1, one_x)
+    one = last_start(1)
     for l in range(2):
         for q in range(PIECES):
             halo_done(l, q)
     for copy in started:
         copy.wait_send()
-    x_first_last(1, one_x, f1_ref)
+    last_finish(1, one, f1_ref)
 
 
 def body(slabs, groups, inputs, pre_acts, out_grad, weight_one, weight_two):
@@ -492,9 +499,9 @@
         pltpu.VMEM((2, 2, chips * own, wide), BF),
         pltpu.VMEM((2, groups, own, cells), BF),
         pltpu.VMEM((channels, cells), BF),
-        pltpu.VMEM((2, PIECES, chips * own, piece), BF),
         pltpu.VMEM((2, PIECES, chips * own, piece), F32),
-        pltpu.VMEM((2, PIECES, chips * own, piece), BF),
+        pltpu.VMEM((2, PIECES, chips * own, piece), F32),
+        pltpu.VMEM((2, PIECES, chips * own, piece), F32),
         pltpu.VMEM((2, PIECES, chips, own, piece), BF),
         pltpu.VMEM((2, PIECES, chips - 1, own, piece), BF),
     ]
@@ -502,8 +509,8 @@
         pltpu.VMEM((ZRUN, runs * share, cut), F32),
         pltpu.VMEM((ZRUN, runs * share, cut), BF),
         pltpu.VMEM((ZRUN - 1, runs * share, cut), BF),
-        pltpu.VMEM((runs, share, cut), F32),
-        pltpu.VMEM((runs - 1, share, cut), F32),
+        pltpu.VMEM((XRUN, halves * share, cut), F32),
+        pltpu.VMEM((XRUN - 1, halves * share, cut), F32),
     ]
     for width in (wide, wide - cut):
         scratch += [
@@ -513,12 +520,12 @@
             pltpu.VMEM((ZRUN, 2 * halves * share, fold(width)), F32),
             pltpu.VMEM((ZRUN, 2 * halves * share, fold(width)), BF),
             pltpu.VMEM((ZRUN - 1, 2 * halves * share, fold(width)), BF),
-            pltpu.VMEM((halves, share, width), F32),
-            pltpu.VMEM((halves - 1, share, width), F32),
+            pltpu.VMEM((halves, share, wide), F32),
+            pltpu.VMEM((halves - 1, share, wide), F32),
         ]
     scratch.append(pltpu.SemaphoreType.DMA((5,)))
     for shape in (
-        (2, PIECES, 2), (3, 2 * chips - 1), (2, PIECES), (2, PIECES, chips - 1), (ZRUN - 1,), (runs - 1,),
+        (2, PIECES, 2), (3, 2 * chips - 1), (2, PIECES), (2, PIECES, chips - 1), (ZRUN - 1,), (XRUN - 1,),
         (2, XRUN - 1), (2, ZRUN - 1), (2, halves - 1),
     ):
         scratch += [pltpu.SemaphoreType.DMA(shape), pltpu.SemaphoreType.DMA(shape)]

time: 62.1 us -> 64.2 us (1.034)
  the two profiles are of different devices: /device:TPU:24 before, /device:TPU:8 now
where the time goes in v7:
time: 64.2 us; the launch traced here: 64.1 us
  Pallas kernels  61.5 us (96%)
  local copies, waits for them, and re-layouts  1.88 us (3%)
    pallas_call x1, Pallas kernels, body(): pl.pallas_call(functools.partial(kernel, slabs, groups, own, height, cut)...  61.5 us
    unnamed x3, local copies, waits for them, and re-layouts  1.88 us

profile of v7, /device:TPU:8, one launch (start us, length us, event | category | flops | bytes accessed | tf_op | source)
XLA Modules:
  0.0 64.1 jit_solution(2418317105941750213)
XLA Ops:
  0.6 61.5 %conv_back.1 = (bf16[32,8,128]{2,1,0:T(8,128)(2,1)S(1)}, f32[27,4,32]{2,1,0:T(4,128)S(1)}, f32[27,4,32]{2,1,0:T(4,128)S(1)}) custom-call(bf16[32,8,128]{2,1,0:T(8,128)(2,1)} %bitcast.15, bf16[32,8,128]{2,1,0:T(8,128)(2,1)} %bitcast.16, bf16[32,8,128]{2,1,0:T(8,128)(2,1)} %bitcast.17, bf16[864,256]{1,0:T(8,128)(2,1)} %bitcast.13, bf16[864,256]{1,0:T(8,128)(2,1)} %bitcast.14), custom_call_target="tpu_custom_call" | custom-call | tf_op jit(solution)/shard_map/conv_back/pallas_call | solution.py:533
  62.2 0.6 copy.12
  62.8 0.6 copy.13
  63.4 0.6 copy.14

commit v8 on v6

--- a/solution.py
+++ b/solution.py
@@ -436,12 +436,12 @@
         build(1, 1, q)
     onward = gather_forward(1, gather_in, gather_rest)
     finish_taps(1)
-    pair = grad_first(1)
-    two = x_first_then(0, two)
     gather_finish(onward + [near_in])
     one_x = x_first(1)
+    pair = grad_first(1)
     reorder(1)
     one_z = z_first()
+    two = x_first_then(0, two)
     grad_own(1)
     parts = [grad_second(1, q, pair[q]) for q in range(PIECES)]
     one_x = x_first_then(1, one_x)

time: 62.1 us -> 62.9 us (1.013)
  Pallas kernels: 59.5 us -> 60.2 us
    pallas_call x1, Pallas kernels: 59.5 us -> 60.2 us  [body(): pl.pallas_call(functools.partial(kernel, slabs, groups, own, height, cut)...]
where the time goes in v8:
time: 62.9 us; the launch traced here: 62.7 us
  Pallas kernels  60.2 us (96%)
  local copies, waits for them, and re-layouts  1.88 us (3%)
  between operations  0.64 us (1%)
    pallas_call x1, Pallas kernels, body(): pl.pallas_call(functools.partial(kernel, slabs, groups, own, height, cut)...  60.2 us
    unnamed x3, local copies, waits for them, and re-layouts  1.88 us

profile of v8, /device:TPU:24, one launch (start us, length us, event | category | flops | bytes accessed | tf_op | source)
XLA Modules:
  0.0 62.7 jit_solution(5035384410691598890)
XLA Ops:
  0.6 60.2 %conv_back.1 = (bf16[32,8,128]{2,1,0:T(8,128)(2,1)S(1)}, f32[27,4,32]{2,1,0:T(4,128)S(1)}, f32[27,4,32]{2,1,0:T(4,128)S(1)}) custom-call(bf16[32,8,128]{2,1,0:T(8,128)(2,1)} %bitcast.15, bf16[32,8,128]{2,1,0:T(8,128)(2,1)} %bitcast.16, bf16[32,8,128]{2,1,0:T(8,128)(2,1)} %bitcast.17, bf16[864,256]{1,0:T(8,128)(2,1)} %bitcast.13, bf16[864,256]{1,0:T(8,128)(2,1)} %bitcast.14), custom_call_target="tpu_custom_call" | custom-call | tf_op jit(solution)/shard_map/conv_back/pallas_call | solution.py:526
  60.9 0.6 %copy.12 = bf16[32,1,8,128]{3,2,1,0:T(8,128)(2,1)} copy(bf16[32,1,8,128]{3,2,1,0:T(8,128)(2,1)S(1)} %bitcast.12) | data formatting | bytes 131072
  61.5 0.6 copy.13
  62.1 0.6 copy.14

commit v9 on v6

--- a/solution.py
+++ b/solution.py
@@ -12,7 +12,7 @@
 F32 = jnp.float32
 ZRUN = 8
 XRUN = 4
-CUT = 384
+CUT = 256
 PIECES = 2
 ORDER = (0, -1, 1)
 TAPS = 27

time: 62.1 us -> 62.5 us (level)
  the two profiles are of different devices: /device:TPU:24 before, /device:TPU:8 now
where the time goes in v9:
time: 62.5 us; the launch traced here: 62.4 us
  Pallas kernels  59.9 us (96%)
  local copies, waits for them, and re-layouts  1.88 us (3%)
  between operations  0.64 us (1%)
    pallas_call x1, Pallas kernels, body(): pl.pallas_call(functools.partial(kernel, slabs, groups, own, height, cut)...  59.9 us
    unnamed x3, local copies, waits for them, and re-layouts  1.88 us

profile of v9, /device:TPU:8, one launch (start us, length us, event | category | flops | bytes accessed | tf_op | source)
XLA Modules:
  0.0 62.4 jit_solution(12691641659395916494)
XLA Ops:
  0.6 59.9 %conv_back.1 = (bf16[32,8,128]{2,1,0:T(8,128)(2,1)S(1)}, f32[27,4,32]{2,1,0:T(4,128)S(1)}, f32[27,4,32]{2,1,0:T(4,128)S(1)}) custom-call(bf16[32,8,128]{2,1,0:T(8,128)(2,1)} %bitcast.15, bf16[32,8,128]{2,1,0:T(8,128)(2,1)} %bitcast.16, bf16[32,8,128]{2,1,0:T(8,128)(2,1)} %bitcast.17, bf16[864,256]{1,0:T(8,128)(2,1)} %bitcast.13, bf16[864,256]{1,0:T(8,128)(2,1)} %bitcast.14), custom_call_target="tpu_custom_call" | custom-call | tf_op jit(solution)/shard_map/conv_back/pallas_call | solution.py:526
  60.5 0.6 %copy.12 = bf16[32,1,8,128]{3,2,1,0:T(8,128)(2,1)} copy(bf16[32,1,8,128]{3,2,1,0:T(8,128)(2,1)S(1)} %bitcast.12) | data formatting | bytes 131072
  61.2 0.6 copy.13
  61.8 0.6 copy.14
